TPU v7x, 128 devices: a whole 4x4x4 slice. The times are simulated.
128 devices in a mesh: gx: 8 (over z, x_hi), gz: 16 (over y, x_lo, core).
Axes of the slice: x: 4 (x_hi: 2, x_lo: 2; x = x_hi * 2 + x_lo), y: 4, z: 4, core: 2. Of those that a mesh axis runs over, the one named last changes fastest.
Arguments:
- field: float32 [3, 256, 256, 512], P(None, ('gx', 'gz')), may hold values from -4 to 4
- atom_vel: float32 [3, 2, 256, 65536], P(None, None, 'gx', 'gz'), may hold values from -6 to 6
- cell_ids: int32 [2, 256, 65536], P(None, 'gx', 'gz'), may hold values from 0 to 31, as said below
- fluid: int32 [2, 256, 65536], P(None, 'gx', 'gz'), may hold values from 0 to 1, as said below
Outputs:
- new_field: float32 [3, 256, 256, 512], P(None, ('gx', 'gz'))
- new_atoms: float32 [3, 2, 256, 65536], P(None, None, 'gx', 'gz')
Inputs may be any that keep to these rules, and one draw needn't show every extreme that they name: `cell_ids`: an atom's cell lies in its own brick's spanwise range. Some intersection cells are wall region, and all atoms in them have fluid 0.
All inputs are finite; a program needn't handle non-finite values.
Results may differ from a plain program's by a relative error of at most 0.000076.
Values sent between devices are 32-bit elements; how exact they have to be, the bound alone decides.
No kernel may reach another device: no remote copies, remote signals or barrier semaphores. Data moves between devices by JAX's collectives and lax.ppermute only.
A program may use at most 192 MiB of HBM per device.

v0:
```python
import functools

import jax
import jax.numpy as jnp
from jax import lax
from jax.experimental import pallas as pl
from jax.experimental.pallas import tpu as pltpu
from jax.sharding import PartitionSpec as P

CZ = 32
OY = 2
LANES = 128
TILE = 8
GROUP = 16
LOW = 16
FIRST = 64
SECOND = 104

VISCOUS = 0.15
COURANT = 0.05
PLATE_SPEED = 1.0

ROW_AXES = ("gx", "gz")


def means_kernel(vel_ref, ids_ref, fluid_ref, out_ref, key_ref, one_ref, *, atoms):
    columns = atoms // LANES
    lane = lax.broadcasted_iota(jnp.int32, (TILE, LANES), 1)

    def window(j):
        return pl.ds(pl.multiple_of(j * LANES, LANES), LANES)

    def prepare(j, carry):
        at = window(j)
        cell = jnp.where(fluid_ref[0, :, at] > 0, ids_ref[0, :, at], -1)
        key_ref[:, at] = cell
        one_ref[:, at] = lax.shift_left(jnp.int32(1), (cell & 3) * 8)
        return carry

    lax.fori_loop(0, columns, prepare, 0, unroll=8)
    out = jnp.zeros((TILE, LANES), jnp.float32)
    for first in range(0, CZ, GROUP):

        def body(j, totals):
            at = window(j)
            cell, one = key_ref[:, at], one_ref[:, at]
            v = [vel_ref[c, 0, :, at] for c in range(3)]
            totals = list(totals)
            for k in range(GROUP):
                hit = cell == first + k
                for c in range(3):
                    totals[3 * k + c] = totals[3 * k + c] + jnp.where(hit, v[c], 0.0)
            quad = lax.shift_right_arithmetic(cell, 2)
            for q in range(GROUP // 4):
                totals[3 * GROUP + q] = totals[3 * GROUP + q] + jnp.where(
                    quad == first // 4 + q, one, 0
                )
            return tuple(totals)

        zero = [jnp.zeros((TILE, LANES), jnp.float32)] * (3 * GROUP)
        zero += [jnp.zeros((TILE, LANES), jnp.int32)] * (GROUP // 4)
        totals = lax.fori_loop(0, columns, body, tuple(zero), unroll=4)
        for k in range(GROUP):
            packed = totals[3 * GROUP + k // 4]
            count = lax.shift_right_logical(packed, (k % 4) * 8) & 255
            count = jnp.sum(count.astype(jnp.float32), axis=1, keepdims=True)
            divisor = jnp.maximum(count, 1.0)
            for c in range(3):
                total = jnp.sum(totals[3 * k + c], axis=1, keepdims=True)
                out = jnp.where(lane == c * CZ + first + k, total / divisor, out)
            out = jnp.where(lane == 3 * CZ + first + k, count, out)
    out_ref[...] = out


def cell_means(vel, ids, fluid):
    _, _, nx, atoms = vel.shape
    assert atoms // LANES < 256
    atom_block = pl.BlockSpec((1, TILE, atoms), lambda r, x: (r, x, 0))
    return pl.pallas_call(
        functools.partial(means_kernel, atoms=atoms),
        grid=(OY, nx // TILE),
        in_specs=[
            pl.BlockSpec((3, 1, TILE, atoms), lambda r, x: (0, r, x, 0)),
            atom_block,
            atom_block,
        ],
        out_specs=pl.BlockSpec((TILE, LANES), lambda r, x: (x, r)),
        out_shape=jax.ShapeDtypeStruct((nx, OY * LANES), jnp.float32),
        scratch_shapes=[pltpu.VMEM((TILE, atoms), jnp.int32)] * 2,
        cost_estimate=pl.CostEstimate(flops=10**8, bytes_accessed=30 * 10**6, transcendentals=0),
        name="cell_means",
    )(vel, ids, fluid)


def constrain_kernel(vel_ref, ids_ref, fluid_ref, new_ref, mean_ref, out_ref, *, atoms):
    delta = new_ref[...] - mean_ref[...]
    for j in range(atoms // LANES):
        at = pl.ds(j * LANES, LANES)
        cell = ids_ref[0, :, at]
        weight = fluid_ref[0, :, at].astype(jnp.float32)
        for c in range(3):
            step = jnp.take_along_axis(delta, cell + c * CZ, axis=1)
            out_ref[c, 0, :, at] = vel_ref[c, 0, :, at] + weight * step


def constrain(vel, ids, fluid, new, mean):
    _, _, nx, atoms = vel.shape
    vel_block = pl.BlockSpec((3, 1, TILE, atoms), lambda r, x: (0, r, x, 0))
    atom_block = pl.BlockSpec((1, TILE, atoms), lambda r, x: (r, x, 0))
    cell_block = pl.BlockSpec((TILE, LANES), lambda r, x: (x, r))
    return pl.pallas_call(
        functools.partial(constrain_kernel, atoms=atoms),
        grid=(OY, nx // TILE),
        in_specs=[vel_block, atom_block, atom_block, cell_block, cell_block],
        out_specs=vel_block,
        out_shape=jax.ShapeDtypeStruct(vel.shape, vel.dtype),
        cost_estimate=pl.CostEstimate(flops=10**7, bytes_accessed=15 * 10**6, transcendentals=0),
        name="constrain",
    )(vel, ids, fluid, new, mean)


def plane_update(read, below, above, plane):
    centre = [read(c, plane) for c in range(3)]
    speed = [COURANT * u for u in centre]
    ahead = [VISCOUS - s for s in speed]
    behind = [VISCOUS + s for s in speed]
    nz = centre[0].shape[-1]
    fresh = []
    for c in range(3):
        u = centre[c]
        along_x = read(c, plane + 1) * ahead[0] + read(c, plane - 1) * behind[0]
        along_y = above(c, plane, u) * ahead[1] + below(c, plane, u) * behind[1]
        along_z = pltpu.roll(u, nz - 1, 1) * ahead[2] + pltpu.roll(u, 1, 1) * behind[2]
        fresh.append((1.0 - 6.0 * VISCOUS) * u + along_x + (along_y + along_z))
    return fresh


def two_steps_kernel(*refs, copies, segments, lo, hi, ny, n_in, low_rows):
    ins, out_ref = refs[:n_in], refs[n_in]
    start_ref, step_ref, new_ref, in_sem, out_sem = refs[n_in + 1 :]
    tiles = (hi - lo) // TILE
    nz = start_ref.shape[-1]

    pending = {}
    for number, (segment, source, plane, at, to, count) in enumerate(copies):
        copy = pltpu.make_async_copy(
            ins[source].at[:, :, pl.ds(at, count), :],
            start_ref.at[:, pl.ds(plane, 2), pl.ds(to, count), :],
            in_sem.at[number],
        )
        copy.start()
        pending.setdefault(segment, []).append(copy)
    outgoing = []
    if low_rows is not None:
        outgoing.append(
            pltpu.make_async_copy(
                ins[low_rows], out_ref.at[:, :, pl.ds(0, TILE), :], out_sem.at[0]
            )
        )
        outgoing[0].start()

    if lo == 0:
        for ref, planes in ((start_ref, 6), (step_ref, 4)):
            ref[:, :, pl.ds(TILE, TILE), :] = jnp.zeros((3, planes, TILE, nz), jnp.float32)
    if hi == ny:
        for ref, planes in ((start_ref, 6), (step_ref, 4)):
            at = pl.ds((tiles + 2) * TILE, TILE)
            ref[0, :, at, :] = jnp.full((planes, TILE, nz), PLATE_SPEED, jnp.float32)
            ref[1:, :, at, :] = jnp.zeros((2, planes, TILE, nz), jnp.float32)

    row = lax.broadcasted_iota(jnp.int32, (TILE, nz), 0)

    def readers(ref, t):
        def tile(c, plane, step):
            at = pl.ds(pl.multiple_of((t + step) * TILE, TILE), TILE)
            return ref[c, plane, at, :]

        def read(c, plane):
            return tile(c, plane, 0)

        def below(c, plane, u):
            return pltpu.roll(jnp.where(row == TILE - 1, tile(c, plane, -1), u), 1, 0)

        def above(c, plane, u):
            return pltpu.roll(jnp.where(row == 0, tile(c, plane, 1), u), TILE - 1, 0)

        return read, below, above

    def first_step(t):
        read, below, above = readers(start_ref, t)
        for plane in range(4):
            fresh = plane_update(read, below, above, plane + 1)
            for c in range(3):
                step_ref[c, plane, pl.ds(pl.multiple_of(t * TILE, TILE), TILE), :] = fresh[c]

    def second_step(t):
        read, below, above = readers(step_ref, t)
        for plane in range(2):
            fresh = plane_update(read, below, above, plane + 1)
            for c in range(3):
                at = pl.ds(pl.multiple_of((t - 2) * TILE, TILE), TILE)
                new_ref[c, plane, at, :] = fresh[c]

    def both_steps(t, carry):
        first_step(t)
        second_step(t - 1)
        return carry

    done_first, done_second = (1 if lo == 0 else 0), 1
    for segment, last_tile in enumerate(segments):
        for copy in pending.get(segment, []):
            copy.wait()
        end_first = tiles + 1 if hi == ny else tiles + 2
        reach_first = min(last_tile - 1, end_first) if segment < len(segments) - 1 else end_first
        reach_second = min(reach_first - 1, tiles + 1)
        while done_first < reach_first and done_second >= done_first:
            done_first += 1
            first_step(done_first)
        head = done_second
        if done_first == done_second + 1:
            begin = done_first + 1
        else:
            while done_first < min(reach_first, done_second + 1):
                done_first += 1
                first_step(done_first)
            begin = done_first + 1
        if reach_first >= begin:
            lax.fori_loop(begin, reach_first + 1, both_steps, 0)
            done_first = reach_first
            done_second = max(done_second, reach_first - 1)
        if segment == len(segments) - 1:
            while done_second < tiles + 1:
                done_second += 1
                second_step(done_second)
        if done_second > head:
            at, count = (head - 1) * TILE, (done_second - head) * TILE
            copy = pltpu.make_async_copy(
                new_ref.at[:, :, pl.ds(at, count), :],
                out_ref.at[:, :, pl.ds(at + (lo if out_ref.shape[2] == ny else 0), count), :],
                out_sem.at[len(outgoing)],
            )
            copy.start()
            outgoing.append(copy)
    for copy in outgoing:
        copy.wait()


def two_steps(own, before, after, lo, hi, ny, cuts=(), into=None, low=None, whole=True):
    nz = own[0][0].shape[-1]
    ins, copies = [], []
    floor, ceiling = max(lo - TILE, 0), min(hi + TILE, ny)
    edges = [floor] + [cut for cut in cuts if floor < cut < ceiling] + [ceiling]
    for plane, pieces in ((0, before), (2, own), (4, after)):
        for array, first in pieces:
            last = first + array.shape[2]
            used = False
            for segment, (a, b) in enumerate(zip(edges[:-1], edges[1:])):
                a, b = max(a, first), min(b, last)
                if a < b:
                    copies.append(
                        (segment, len(ins), plane, a - first, a - lo + 2 * TILE, b - a)
                    )
                    used = True
            if used:
                ins.append(array)
    segments = [(edge - lo) // TILE + 1 for edge in edges[1:]]
    low_rows = None
    if low is not None:
        low_rows = len(ins)
        ins.append(low)
    aliases = {}
    if into is not None:
        aliases = {len(ins): 0}
        ins.append(into)
    copies.sort(key=lambda copy: copy[0])
    span = hi - lo
    anywhere = pl.BlockSpec(memory_space=pl.ANY)
    return pl.pallas_call(
        functools.partial(
            two_steps_kernel,
            copies=copies,
            segments=segments,
            lo=lo,
            hi=hi,
            ny=ny,
            n_in=len(ins),
            low_rows=low_rows,
        ),
        in_specs=[anywhere] * len(ins),
        out_specs=anywhere,
        out_shape=jax.ShapeDtypeStruct((3, 2, ny if whole else span, nz), jnp.float32),
        scratch_shapes=[
            pltpu.VMEM((3, 6, span + 4 * TILE, nz), jnp.float32),
            pltpu.VMEM((3, 4, span + 4 * TILE, nz), jnp.float32),
            pltpu.VMEM((3, 2, span, nz), jnp.float32),
            pltpu.SemaphoreType.DMA((len(copies),)),
            pltpu.SemaphoreType.DMA((len(segments) + 1,)),
        ],
        input_output_aliases=aliases,
        compiler_params=pltpu.CompilerParams(vmem_limit_bytes=40 * 2**20),
        cost_estimate=pl.CostEstimate(
            flops=span * 10**6, bytes_accessed=span * 60 * 10**3, transcendentals=0
        ),
        name="two_steps",
    )(*ins)


def tie(value, *others):
    return lax.optimization_barrier((value,) + others)[0]


def local(field, atom_vel, cell_ids, fluid):
    _, planes, ny, nz = field.shape
    nx = atom_vel.shape[2]
    blocks = nz // CZ
    count = lax.axis_size("gx") * lax.axis_size("gz")
    forward = [(i, (i + 1) % count) for i in range(count)]
    backward = [(target, source) for source, target in forward]

    def halo(block):
        return lax.ppermute(block, ROW_AXES, forward), lax.ppermute(block, ROW_AXES, backward)

    first = halo(field[:, :, LOW:FIRST])
    means = cell_means(atom_vel, cell_ids, fluid)
    slab = lax.all_to_all(means, "gz", split_axis=0, concat_axis=0, tiled=True)
    second = halo(tie(field[:, :, FIRST:SECOND], slab))
    slab = slab.reshape(blocks, planes, OY, 4, CZ).transpose(3, 1, 2, 0, 4)
    slab = slab.reshape(4, planes, OY, nz)
    seeded = jnp.where(slab[3:] > 0, slab[:3], field[:, :, :OY])
    base = jnp.concatenate([seeded, field[:, :, OY:LOW]], 2)
    bottom = halo(base)
    own = [(base, 0), (field[:, :, LOW:], LOW)]
    low = two_steps(
        [(base, 0)], [(bottom[0], 0)], [(bottom[1], 0)], 0, TILE, ny, whole=False
    )
    back = low[:, :, :OY].reshape(3, planes, OY, blocks, CZ).transpose(3, 1, 2, 0, 4)
    back = jnp.pad(back, ((0, 0),) * 3 + ((0, 1), (0, 0))).reshape(blocks * planes, OY * LANES)
    back = lax.all_to_all(back, "gz", split_axis=0, concat_axis=0, tiled=True)
    third = halo(tie(field[:, :, SECOND:], back))
    new_atoms = constrain(atom_vel, cell_ids, fluid, back, means)

    before = [(bottom[0], 0), (first[0], LOW), (second[0], FIRST), (third[0], SECOND)]
    after = [(bottom[1], 0), (first[1], LOW), (second[1], FIRST), (third[1], SECOND)]
    part = two_steps([(field, 0)], before[:3], after[:3], TILE, SECOND - TILE, ny, (40, 72))
    new_field = two_steps(
        [(field, 0)],
        before[1:],
        after[1:],
        SECOND - TILE,
        ny,
        ny,
        (136, 176, 216),
        into=part,
        low=low,
    )
    return new_field, new_atoms


def solution(mesh):
    placed = (
        P(None, ("gx", "gz"), None, None),
        P(None, None, "gx", "gz"),
        P(None, "gx", "gz"),
        P(None, "gx", "gz"),
    )
    return jax.shard_map(
        local,
        mesh=mesh,
        in_specs=placed,
        out_specs=(P(None, ("gx", "gz"), None, None), P(None, None, "gx", "gz")),
        check_vma=False,
    )
```

profile of v0, /device:TPU:3, one launch (start us, length us, event | category | flops | bytes accessed | tf_op | source)
XLA Modules:
  0.0 148.6 jit_solution(1783038941696087946)
XLA Ops:
  0.6 14.9 %cell_means.1.mean_ref = f32[32,256]{1,0:T(8,128)} custom-call(f32[3,2,32,4096]{3,2,1,0:T(8,128)} %vel_ref.3, s32[2,32,4096]{2,1,0:T(8,128)} %ids_ref.3, s32[2,32,4096]{2,1,0:T(8,128)} %fluid_ref.3), custom_call_target="tpu_custom_call" | custom-call | flops 100000000 | bytes 30000000 | tf_op jit(solution)/shard_map/cell_means/pallas_call | solution.py:79
  15.6 1.4 all_to_all.13
  17.0 6.3 %all-to-all-start = ((f32[16,2,256]{2,1,0:T(2,128)}), f32[16,2,256]{2,1,0:T(2,128)S(1)}, u32[]{:S(2)}, u32[]{:S(2)}) async-start(f32[16,2,256]{2,1,0:T(2,128)} %all_to_all.13), calls=%async_computation | async-start | bytes 65536 | tf_op jit(solution)/shard_map/all_to_all | solution.py:325
  23.2 4.7 %all-to-all-done = f32[16,2,256]{2,1,0:T(2,128)S(1)} async-done(((f32[16,2,256]{2,1,0:T(2,128)}), f32[16,2,256]{2,1,0:T(2,128)S(1)}, u32[]{:S(2)}, u32[]{:S(2)}) %all-to-all-start) | async-done | bytes 32800 | tf_op jit(solution)/shard_map/all_to_all | solution.py:325
  28.0 0.8 reshape.31
  28.8 0.9 copy.26
  29.7 0.6 slice.38
  30.4 1.0 slice.32
  32.0 2.2 %collective-permute-start.1 = (f32[3,2,16,512]{3,2,1,0:T(8,128)S(1)}, f32[3,2,16,512]{3,2,1,0:T(8,128)S(1)}, u32[]{:S(2)}, u32[]{:S(2)}) collective-permute-start(f32[3,2,16,512]{3,2,1,0:T(8,128)S(1)} %pad_maximum_fusion.refs_1_), channel_id=1, source_target_pairs={{0,1},{1,2},{2,3},{3,4},{4,5},{5,6},{6,7},{7,8},{8,9},{9,10},{10,1... | collective-permute-start | bytes 589832 | tf_op jit(solution)/shard_map/ppermute | solution.py:321
  34.2 5.4 %collective-permute-done.2.refs_2_.refs_4_ = f32[3,2,16,512]{3,2,1,0:T(8,128)S(1)} collective-permute-done((f32[3,2,16,512]{3,2,1,0:T(8,128)S(1)}, f32[3,2,16,512]{3,2,1,0:T(8,128)S(1)}, u32[]{:S(2)}, u32[]{:S(2)}) %collective-permute-start.2) | collective-permute-done | bytes 196640 | tf_op jit(solution)/shard_map/ppermute | solution.py:321
  39.6 0.6 two_steps.3.refs_5_
  40.9 0.6 copy-done.3
  41.5 1.5 reshape.30
  43.0 1.0 copy.24
  44.0 0.7 pad.4.clone
  44.6 1.7 %all_to_all.15 = f32[16,2,256]{2,1,0:T(2,128)} reshape(f32[16,2,2,4,32]{4,3,2,1,0:T(4,128)} %pad.4.clone) | data formatting | bytes 65536 | tf_op jit(solution)/shard_map/all_to_all | solution.py:338
  46.3 13.5 %all-to-all-start.1 = ((f32[16,2,256]{2,1,0:T(2,128)}), f32[16,2,256]{2,1,0:T(2,128)}, u32[]{:S(2)}, u32[]{:S(2)}) async-start(f32[16,2,256]{2,1,0:T(2,128)} %all_to_all.15), calls=%async_computation.1 | async-start | bytes 65536 | tf_op jit(solution)/shard_map/all_to_all | solution.py:338
  59.8 1.5 %slice.29 = f32[3,2,152,512]{3,2,1,0:T(8,128)} slice(f32[3,2,256,512]{3,2,1,0:T(8,128)S(1)} %copy-done), slice={[0:3], [0:2], [104:256], [0:512]} | slice | bytes 3735552 | tf_op jit(solution)/shard_map/slice | solution.py:339
  61.3 3.4 %all-to-all-done.1 = f32[16,2,256]{2,1,0:T(2,128)} async-done(((f32[16,2,256]{2,1,0:T(2,128)}), f32[16,2,256]{2,1,0:T(2,128)}, u32[]{:S(2)}, u32[]{:S(2)}) %all-to-all-start.1) | async-done | bytes 32800 | tf_op jit(solution)/shard_map/all_to_all | solution.py:338
  64.7 1.4 all_to_all.17.new_ref
  66.4 2.2 %collective-permute-start.3 = (f32[3,2,152,512]{3,2,1,0:T(8,128)}, f32[3,2,152,512]{3,2,1,0:T(8,128)}, u32[]{:S(2)}, u32[]{:S(2)}) collective-permute-start(f32[3,2,152,512]{3,2,1,0:T(8,128)} %slice.29), channel_id=1, source_target_pairs={{0,1},{1,2},{2,3},{3,4},{4,5},{5,6},{6,7},{7,8},{8,9},{9,10},{10,1... | collective-permute-start | bytes 5603336 | tf_op jit(solution)/shard_map/ppermute | solution.py:321
  68.7 0.8 slice.28
  69.5 0.9 slice.36
  71.0 2.0 %collective-permute-start.6 = (f32[3,2,48,512]{3,2,1,0:T(8,128)}, f32[3,2,48,512]{3,2,1,0:T(8,128)}, u32[]{:S(2)}, u32[]{:S(2)}) collective-permute-start(f32[3,2,48,512]{3,2,1,0:T(8,128)} %slice.36), channel_id=1, source_target_pairs={{0,1},{1,2},{2,3},{3,4},{4,5},{5,6},{6,7},{7,8},{8,9},{9,10},{10,1... | collective-permute-start | bytes 1769480 | tf_op jit(solution)/shard_map/ppermute | solution.py:321
  73.0 47.7 %collective-permute-done.4.refs_6_.refs_3_ = f32[3,2,40,512]{3,2,1,0:T(8,128)S(1)} collective-permute-done((f32[3,2,40,512]{3,2,1,0:T(8,128)}, f32[3,2,40,512]{3,2,1,0:T(8,128)S(1)}, u32[]{:S(2)}, u32[]{:S(2)}) %collective-permute-start.4) | collective-permute-done | bytes 491552 | tf_op jit(solution)/shard_map/ppermute | solution.py:321
  120.7 0.8 copy-done.1
  121.5 7.6 %constrain.1 = f32[3,2,32,4096]{3,2,1,0:T(8,128)} custom-call(f32[3,2,32,4096]{3,2,1,0:T(8,128)} %vel_ref.3, s32[2,32,4096]{2,1,0:T(8,128)} %ids_ref.3, s32[2,32,4096]{2,1,0:T(8,128)} %fluid_ref.3, f32[32,256]{1,0:T(8,128)} %all_to_all.17.new_ref, f32[32,256]{1,0:T(8,128)} %cell_means.1.mean_ref), custom_call_target="tpu_custom_call" | custom-call | flops 10000000 | bytes 15000000 | tf_op jit(solution)/shard_map/constrain/pallas_call | solution.py:111
  129.1 2.6 %collective-permute-done.refs_2_.refs_0_ = f32[3,2,40,512]{3,2,1,0:T(8,128)} collective-permute-done((f32[3,2,40,512]{3,2,1,0:T(8,128)}, f32[3,2,40,512]{3,2,1,0:T(8,128)}, u32[]{:S(2)}, u32[]{:S(2)}) %collective-permute-start) | collective-permute-done | bytes 491552 | tf_op jit(solution)/shard_map/ppermute | solution.py:321
  131.8 1.6 %collective-permute-done.7.refs_5_ = f32[3,2,48,512]{3,2,1,0:T(8,128)} collective-permute-done((f32[3,2,48,512]{3,2,1,0:T(8,128)}, f32[3,2,48,512]{3,2,1,0:T(8,128)}, u32[]{:S(2)}, u32[]{:S(2)}) %collective-permute-start.7) | collective-permute-done | bytes 589856 | tf_op jit(solution)/shard_map/ppermute | solution.py:321
  133.4 1.0 copy-done.2
  134.5 5.7 %two_steps.4.refs_6_ = f32[3,2,256,512]{3,2,1,0:T(8,128)} custom-call(f32[3,2,16,512]{3,2,1,0:T(8,128)S(1)} %collective-permute-done.1.refs_0_, f32[3,2,48,512]{3,2,1,0:T(8,128)} %collective-permute-done.6.refs_1_, f32[3,2,40,512]{3,2,1,0:T(8,128)} %collective-permute-done.refs_2_.refs_0_, f32[3,2,256,512]{3,2,1,0:T(8,128)S(1)} %copy-done, ...), custom_call_target="tpu_custom_call" | custom-call | flops 88000000 | bytes 5280000 | tf_op jit(solution)/shard_map/two_steps/pallas_call | solution.py:278
  140.2 8.4 %two_steps.5 = f32[3,2,256,512]{3,2,1,0:T(8,128)} custom-call(f32[3,2,40,512]{3,2,1,0:T(8,128)} %collective-permute-done.refs_2_.refs_0_, f32[3,2,152,512]{3,2,1,0:T(8,128)} %collective-permute-done.3.refs_1_, f32[3,2,256,512]{3,2,1,0:T(8,128)S(1)} %copy-done, f32[3,2,40,512]{3,2,1,0:T(8,128)S(1)} %copy-done.2, ...), custom_call_target="tpu_custom_call", output_to_operand_aliasing={{}: (6, {})} | custom-call | flops 160000000 | bytes 9600000 | tf_op jit(solution)/shard_map/two_steps/pallas_call | solution.py:278
  (22 shorter events, 2.3 us)
Async XLA Ops:
  0.6 22.6 %copy-start = (f32[3,2,256,512]{3,2,1,0:T(8,128)S(1)}, f32[3,2,256,512]{3,2,1,0:T(8,128)}, u32[]{:S(2)}) copy-start(f32[3,2,256,512]{3,2,1,0:T(8,128)} %refs_2_.1) | copy-start | bytes 9437188
  17.0 11.0 %all-to-all-start = ((f32[16,2,256]{2,1,0:T(2,128)}), f32[16,2,256]{2,1,0:T(2,128)S(1)}, u32[]{:S(2)}, u32[]{:S(2)}) async-start(f32[16,2,256]{2,1,0:T(2,128)} %all_to_all.13), calls=%async_computation | async-start | bytes 65536 | tf_op jit(solution)/shard_map/all_to_all | solution.py:325
  31.5 8.1 %collective-permute-start.2 = (f32[3,2,16,512]{3,2,1,0:T(8,128)S(1)}, f32[3,2,16,512]{3,2,1,0:T(8,128)S(1)}, u32[]{:S(2)}, u32[]{:S(2)}) collective-permute-start(f32[3,2,16,512]{3,2,1,0:T(8,128)S(1)} %pad_maximum_fusion.refs_1_), channel_id=1, source_target_pairs={{1,0},{2,1},{3,2},{4,3},{5,4},{6,5},{7,6},{8,7},{9,8},{10,9},{11,1... | collective-permute-start | bytes 589832 | tf_op jit(solution)/shard_map/ppermute | solution.py:321
  32.0 7.6 %collective-permute-start.1 = (f32[3,2,16,512]{3,2,1,0:T(8,128)S(1)}, f32[3,2,16,512]{3,2,1,0:T(8,128)S(1)}, u32[]{:S(2)}, u32[]{:S(2)}) collective-permute-start(f32[3,2,16,512]{3,2,1,0:T(8,128)S(1)} %pad_maximum_fusion.refs_1_), channel_id=1, source_target_pairs={{0,1},{1,2},{2,3},{3,4},{4,5},{5,6},{6,7},{7,8},{8,9},{9,10},{10,1... | collective-permute-start | bytes 589832 | tf_op jit(solution)/shard_map/ppermute | solution.py:321
  40.9 0.6 copy-start.3
  46.3 18.4 %all-to-all-start.1 = ((f32[16,2,256]{2,1,0:T(2,128)}), f32[16,2,256]{2,1,0:T(2,128)}, u32[]{:S(2)}, u32[]{:S(2)}) async-start(f32[16,2,256]{2,1,0:T(2,128)} %all_to_all.15), calls=%async_computation.1 | async-start | bytes 65536 | tf_op jit(solution)/shard_map/all_to_all | solution.py:338
  66.1 74.1 %collective-permute-start.5 = (f32[3,2,152,512]{3,2,1,0:T(8,128)}, f32[3,2,152,512]{3,2,1,0:T(8,128)}, u32[]{:S(2)}, u32[]{:S(2)}) collective-permute-start(f32[3,2,152,512]{3,2,1,0:T(8,128)} %slice.29), channel_id=1, source_target_pairs={{1,0},{2,1},{3,2},{4,3},{5,4},{6,5},{7,6},{8,7},{9,8},{10,9},{11,1... | collective-permute-start | bytes 5603336 | tf_op jit(solution)/shard_map/ppermute | solution.py:321
  66.4 73.7 %collective-permute-start.3 = (f32[3,2,152,512]{3,2,1,0:T(8,128)}, f32[3,2,152,512]{3,2,1,0:T(8,128)}, u32[]{:S(2)}, u32[]{:S(2)}) collective-permute-start(f32[3,2,152,512]{3,2,1,0:T(8,128)} %slice.29), channel_id=1, source_target_pairs={{0,1},{1,2},{2,3},{3,4},{4,5},{5,6},{6,7},{7,8},{8,9},{9,10},{10,1... | collective-permute-start | bytes 5603336 | tf_op jit(solution)/shard_map/ppermute | solution.py:321
  69.5 51.2 %collective-permute-start.4 = (f32[3,2,40,512]{3,2,1,0:T(8,128)}, f32[3,2,40,512]{3,2,1,0:T(8,128)S(1)}, u32[]{:S(2)}, u32[]{:S(2)}) collective-permute-start(f32[3,2,40,512]{3,2,1,0:T(8,128)} %slice.28), channel_id=1, source_target_pairs={{1,0},{2,1},{3,2},{4,3},{5,4},{6,5},{7,6},{8,7},{9,8},{10,9},{11,1... | collective-permute-start | bytes 1474568 | tf_op jit(solution)/shard_map/ppermute | solution.py:321
  70.4 63.0 %collective-permute-start.7 = (f32[3,2,48,512]{3,2,1,0:T(8,128)}, f32[3,2,48,512]{3,2,1,0:T(8,128)}, u32[]{:S(2)}, u32[]{:S(2)}) collective-permute-start(f32[3,2,48,512]{3,2,1,0:T(8,128)} %slice.36), channel_id=1, source_target_pairs={{1,0},{2,1},{3,2},{4,3},{5,4},{6,5},{7,6},{8,7},{9,8},{10,9},{11,1... | collective-permute-start | bytes 1769480 | tf_op jit(solution)/shard_map/ppermute | solution.py:321
  71.0 62.4 %collective-permute-start.6 = (f32[3,2,48,512]{3,2,1,0:T(8,128)}, f32[3,2,48,512]{3,2,1,0:T(8,128)}, u32[]{:S(2)}, u32[]{:S(2)}) collective-permute-start(f32[3,2,48,512]{3,2,1,0:T(8,128)} %slice.36), channel_id=1, source_target_pairs={{0,1},{1,2},{2,3},{3,4},{4,5},{5,6},{6,7},{7,8},{8,9},{9,10},{10,1... | collective-permute-start | bytes 1769480 | tf_op jit(solution)/shard_map/ppermute | solution.py:321
  120.7 0.8 copy-start.1
  121.5 10.2 %collective-permute-start = (f32[3,2,40,512]{3,2,1,0:T(8,128)}, f32[3,2,40,512]{3,2,1,0:T(8,128)}, u32[]{:S(2)}, u32[]{:S(2)}) collective-permute-start(f32[3,2,40,512]{3,2,1,0:T(8,128)} %slice.28), channel_id=1, source_target_pairs={{0,1},{1,2},{2,3},{3,4},{4,5},{5,6},{6,7},{7,8},{8,9},{9,10},{10,1... | collective-permute-start | bytes 1474568 | tf_op jit(solution)/shard_map/ppermute | solution.py:321
  133.4 1.0 copy-start.2
  134.5 5.7 %copy-start.4 = (f32[3,2,8,512]{3,2,1,0:T(8,128)S(1)}, f32[3,2,8,512]{3,2,1,0:T(8,128)}, u32[]{:S(2)}) copy-start(f32[3,2,8,512]{3,2,1,0:T(8,128)} %copy-done.3) | copy-start | bytes 294916
where the time goes:
time: 149 us
  waiting for transfers between devices  65.5 us (44%)
  Pallas kernels  37.3 us (25%)
  starting transfers between devices  27.7 us (19%)
  local copies, waits for them, and re-layouts  17.4 us (12%)
    ppermute x4, waiting for transfers between devices, halo(): lax.ppermute(block, ROW_AXES, backward)  54.7 us
    pallas_call x1, Pallas kernels, cell_means(): pl.pallas_call(functools.partial(means_kernel, atoms=atoms), grid=(OY, nx...  14.9 us
    pallas_call x3, Pallas kernels, two_steps(): pl.pallas_call(functools.partial(two_steps_kernel, copies=copies, segment...  14.8 us
    all_to_all x1, starting transfers between devices, local(): back = lax.all_to_all(back, 'gz', split_axis=0, concat_axis=0, tiled=True)  13.5 us
    pallas_call x1, Pallas kernels, constrain(): pl.pallas_call(functools.partial(constrain_kernel, atoms=atoms), grid=(OY...  7.59 us
    ppermute x4, starting transfers between devices, halo(): lax.ppermute(block, ROW_AXES, forward)  6.52 us
    all_to_all x1, starting transfers between devices, local(): slab = lax.all_to_all(means, 'gz', split_axis=0, concat_axis=0, tiled=True)  6.26 us
    all_to_all x1, waiting for transfers between devices, local(): slab = lax.all_to_all(means, 'gz', split_axis=0, concat_axis=0, tiled=True)  4.73 us
  transfers between devices with their start and end apart: 10, of which 6 were waited for; matrix products, arithmetic and copies ran while one was open for 2% of the time, Pallas kernels for 9%

commit v1 on v0

v1 whole, which is shorter than its diff:
```python
import functools

import jax
import jax.numpy as jnp
from jax import lax
from jax.experimental import pallas as pl
from jax.experimental.pallas import tpu as pltpu
from jax.sharding import PartitionSpec as P

CZ = 32
OY = 2
LANES = 128
TILE = 8
GROUP = 16
VMEM_BYTES = 64 * 2**20
LOW = 8
FIRST = 112
SECOND = 168
THIRD = 232

VISCOUS = 0.15
COURANT = 0.05
PLATE_SPEED = 1.0

ROW_AXES = ("gx", "gz")


def means_kernel(vel_ref, ids_ref, fluid_ref, field_ref, out_ref, send_ref, *refs, atoms, cuts):
    pieces, (key_ref, one_ref, held_ref, sem) = refs[:-4], refs[-4:]
    fetch = pltpu.make_async_copy(
        field_ref.at[:, :, pl.ds(cuts[0], cuts[-1] - cuts[0]), :], held_ref, sem.at[len(pieces)]
    )
    copies = [
        pltpu.make_async_copy(
            held_ref.at[:, :, pl.ds(a - cuts[0], b - a), :], piece, sem.at[number]
        )
        for number, (a, b, piece) in enumerate(zip(cuts[:-1], cuts[1:], pieces))
    ]

    @pl.when(pl.program_id(0) == 0)
    def _():
        fetch.start()

    @pl.when(pl.program_id(0) == 1)
    def _():
        fetch.wait()
        for copy in copies:
            copy.start()

    columns = atoms // LANES
    lane = lax.broadcasted_iota(jnp.int32, (TILE, LANES), 1)

    def window(j):
        return pl.ds(pl.multiple_of(j * LANES, LANES), LANES)

    for r in range(OY):

        def prepare(j, carry):
            at = window(j)
            cell = jnp.where(fluid_ref[r, :, at] > 0, ids_ref[r, :, at], -1)
            key_ref[:, at] = cell
            one_ref[:, at] = lax.shift_left(jnp.int32(1), (cell & 3) * 8)
            return carry

        lax.fori_loop(0, columns, prepare, 0, unroll=8)
        out = jnp.zeros((TILE, LANES), jnp.float32)
        for first in range(0, CZ, GROUP):

            def body(j, totals):
                at = window(j)
                cell, one = key_ref[:, at], one_ref[:, at]
                v = [vel_ref[c, r, :, at] for c in range(3)]
                totals = list(totals)
                for k in range(GROUP):
                    hit = cell == first + k
                    for c in range(3):
                        totals[3 * k + c] = totals[3 * k + c] + jnp.where(hit, v[c], 0.0)
                quad = lax.shift_right_arithmetic(cell, 2)
                for q in range(GROUP // 4):
                    totals[3 * GROUP + q] = totals[3 * GROUP + q] + jnp.where(
                        quad == first // 4 + q, one, 0
                    )
                return tuple(totals)

            zero = [jnp.zeros((TILE, LANES), jnp.float32)] * (3 * GROUP)
            zero += [jnp.zeros((TILE, LANES), jnp.int32)] * (GROUP // 4)
            totals = lax.fori_loop(0, columns, body, tuple(zero), unroll=4)
            for k in range(GROUP):
                packed = totals[3 * GROUP + k // 4]
                count = lax.shift_right_logical(packed, (k % 4) * 8) & 255
                count = jnp.sum(count.astype(jnp.float32), axis=1, keepdims=True)
                divisor = jnp.maximum(count, 1.0)
                for c in range(3):
                    total = jnp.sum(totals[3 * k + c], axis=1, keepdims=True)
                    out = jnp.where(lane == c * CZ + first + k, total / divisor, out)
                out = jnp.where(lane == 3 * CZ + first + k, count, out)
        out_ref[:, pl.ds(r * LANES, LANES)] = out
        for x in range(TILE):
            send_ref[x // 2, pl.ds((x % 2) * OY + r, 1), :] = out[x : x + 1]
            send_ref[x // 2, pl.ds(4 + (x % 2) * OY + r, 1), :] = out[x : x + 1]

    @pl.when(pl.program_id(0) == pl.num_programs(0) - 1)
    def _():
        for copy in copies:
            copy.wait()


def cell_means(vel, ids, fluid, field, cuts):
    _, _, nx, atoms = vel.shape
    assert atoms // LANES < 256 and nx >= 2 * TILE
    atom_block = pl.BlockSpec((OY, TILE, atoms), lambda x: (0, x, 0))
    return pl.pallas_call(
        functools.partial(means_kernel, atoms=atoms, cuts=cuts),
        grid=(nx // TILE,),
        in_specs=[
            pl.BlockSpec((3, OY, TILE, atoms), lambda x: (0, 0, x, 0)),
            atom_block,
            atom_block,
            pl.BlockSpec(memory_space=pltpu.HBM),
        ],
        out_specs=[
            pl.BlockSpec((TILE, OY * LANES), lambda x: (x, 0)),
            pl.BlockSpec((TILE // 2, 8, LANES), lambda x: (x, 0, 0)),
        ]
        + [pl.BlockSpec(memory_space=pltpu.HBM)] * (len(cuts) - 1),
        out_shape=[
            jax.ShapeDtypeStruct((nx, OY * LANES), jnp.float32),
            jax.ShapeDtypeStruct((nx // 2, 8, LANES), jnp.float32),
        ]
        + [
            jax.ShapeDtypeStruct((3, 2, b - a, field.shape[3]), jnp.float32)
            for a, b in zip(cuts[:-1], cuts[1:])
        ],
        scratch_shapes=[pltpu.VMEM((TILE, atoms), jnp.int32)] * 2
        + [
            pltpu.VMEM((3, 2, cuts[-1] - cuts[0], field.shape[3]), jnp.float32),
            pltpu.SemaphoreType.DMA((len(cuts),)),
        ],
        compiler_params=pltpu.CompilerParams(vmem_limit_bytes=VMEM_BYTES),
        cost_estimate=pl.CostEstimate(flops=10**8, bytes_accessed=40 * 10**6, transcendentals=0),
        name="cell_means",
    )(vel, ids, fluid, field)


def spread(block, k):
    return pltpu.roll(block, k % 4 * CZ, 1) if k % 4 else block


def seed_kernel(slab_ref, field_ref, out_ref):
    lane = lax.broadcasted_iota(jnp.int32, (TILE, LANES), 1) // CZ
    source = lax.broadcasted_iota(jnp.int32, (TILE, LANES), 0) // 2
    for q in range(slab_ref.shape[0] // 4):
        at = pl.ds(q * LANES, LANES)
        for r in range(OY):
            rows = [slab_ref[4 * q + m, pl.ds(p * OY + r, 1), :] for m in range(4) for p in range(2)]
            block = jnp.concatenate(rows, 0)
            turned = [spread(block, k) for k in range(4)]
            whole = []
            for c in range(4):
                part = jnp.zeros((TILE, LANES), jnp.float32)
                for m in range(4):
                    mine = jnp.logical_and(source == m, lane == m)
                    part = jnp.where(mine, turned[(m - c) % 4], part)
                part = part + pltpu.roll(part, 4, 0)
                whole.append(part + pltpu.roll(part, 2, 0))
            for c in range(3):
                for p in range(2):
                    kept = field_ref[c, p, pl.ds(r, 1), at]
                    fresh = jnp.where(whole[3][p : p + 1] > 0, whole[c][p : p + 1], kept)
                    out_ref[c, p, pl.ds(r, 1), at] = fresh
    out_ref[:, :, pl.ds(OY, LOW - OY), :] = field_ref[:, :, pl.ds(OY, LOW - OY), :]


def seed(slab, field):
    block = pl.BlockSpec((3, 2, LOW, field.shape[3]), lambda i: (0, 0, 0, 0))
    return pl.pallas_call(
        seed_kernel,
        grid=(1,),
        in_specs=[pl.BlockSpec(slab.shape, lambda i: (0, 0, 0)), block],
        out_specs=block,
        out_shape=jax.ShapeDtypeStruct((3, 2, LOW, field.shape[3]), jnp.float32),
        compiler_params=pltpu.CompilerParams(vmem_limit_bytes=VMEM_BYTES),
        name="seed",
    )(slab, field)


def write_back(low_ref, out_ref):
    lane = lax.broadcasted_iota(jnp.int32, (TILE, LANES), 1) // CZ
    row = lax.broadcasted_iota(jnp.int32, (TILE, LANES), 0)
    for q in range(out_ref.shape[0] // 4):
        at = pl.ds(q * LANES, LANES)
        for r in range(OY):
            block = jnp.zeros((TILE, LANES), jnp.float32)
            for c in range(3):
                even, odd = (low_ref[c, p, pl.ds(r, 1), at] for p in range(2))
                both = jnp.where(row % 2 == 0, even, odd)
                for m in range(4):
                    mine = jnp.logical_and(row // 2 == m, lane == c)
                    block = jnp.where(mine, spread(both, c - m), block)
            for m in range(4):
                for p in range(2):
                    line = block[2 * m + p : 2 * m + p + 1]
                    out_ref[4 * q + m, pl.ds(p * OY + r, 1), :] = line
                    out_ref[4 * q + m, pl.ds(4 + p * OY + r, 1), :] = line


def constrain_kernel(vel_ref, ids_ref, fluid_ref, new_ref, mean_ref, out_ref, *, atoms):
    for r in range(OY):
        rows = [new_ref[x // 2, pl.ds((x % 2) * OY + r, 1), :] for x in range(TILE)]
        delta = jnp.concatenate(rows, 0) - mean_ref[:, pl.ds(r * LANES, LANES)]
        for j in range(atoms // LANES):
            at = pl.ds(j * LANES, LANES)
            cell = ids_ref[r, :, at]
            weight = fluid_ref[r, :, at].astype(jnp.float32)
            for c in range(3):
                step = jnp.take_along_axis(delta, cell + c * CZ, axis=1)
                out_ref[c, r, :, at] = vel_ref[c, r, :, at] + weight * step


def constrain(vel, ids, fluid, new, mean):
    _, _, nx, atoms = vel.shape
    vel_block = pl.BlockSpec((3, OY, TILE, atoms), lambda x: (0, 0, x, 0))
    atom_block = pl.BlockSpec((OY, TILE, atoms), lambda x: (0, x, 0))
    return pl.pallas_call(
        functools.partial(constrain_kernel, atoms=atoms),
        grid=(nx // TILE,),
        in_specs=[
            vel_block,
            atom_block,
            atom_block,
            pl.BlockSpec((TILE // 2, 8, LANES), lambda x: (x, 0, 0)),
            pl.BlockSpec((TILE, OY * LANES), lambda x: (x, 0)),
        ],
        out_specs=vel_block,
        out_shape=jax.ShapeDtypeStruct(vel.shape, vel.dtype),
        compiler_params=pltpu.CompilerParams(vmem_limit_bytes=VMEM_BYTES),
        cost_estimate=pl.CostEstimate(flops=10**7, bytes_accessed=20 * 10**6, transcendentals=0),
        name="constrain",
    )(vel, ids, fluid, new, mean)


def plane_update(read, below, above, plane):
    centre = [read(c, plane) for c in range(3)]
    speed = [COURANT * u for u in centre]
    ahead = [VISCOUS - s for s in speed]
    behind = [VISCOUS + s for s in speed]
    nz = centre[0].shape[-1]
    fresh = []
    for c in range(3):
        u = centre[c]
        along_x = read(c, plane + 1) * ahead[0] + read(c, plane - 1) * behind[0]
        along_y = above(c, plane, u) * ahead[1] + below(c, plane, u) * behind[1]
        along_z = pltpu.roll(u, nz - 1, 1) * ahead[2] + pltpu.roll(u, 1, 1) * behind[2]
        fresh.append((1.0 - 6.0 * VISCOUS) * u + along_x + (along_y + along_z))
    return fresh


def two_steps_kernel(*refs, copies, segments, lo, hi, ny, n_in, low_rows):
    core_ref, ins, out_ref = refs[0], refs[1 : n_in + 1], refs[n_in + 1]
    start_ref, step_ref, new_ref, in_sem, out_sem = refs[-5:]
    tiles = (hi - lo) // TILE
    nz = start_ref.shape[-1]
    place = {"own": 2, "chip": 4 - 4 * core_ref[0], "far": 4 * core_ref[0]}

    pending = {}
    for number, (segment, source, plane, at, to, count) in enumerate(copies):
        copy = pltpu.make_async_copy(
            ins[source].at[:, :, pl.ds(at, count), :],
            start_ref.at[:, pl.ds(place[plane], 2), pl.ds(to, count), :],
            in_sem.at[number],
        )
        copy.start()
        pending.setdefault(segment, []).append(copy)
    outgoing = []
    if low_rows is not None:
        outgoing.append(
            pltpu.make_async_copy(
                ins[low_rows], out_ref.at[:, :, pl.ds(0, TILE), :], out_sem.at[0]
            )
        )
        outgoing[0].start()

    if lo == 0:
        for ref, planes in ((start_ref, 6), (step_ref, 4)):
            ref[:, :, pl.ds(TILE, TILE), :] = jnp.zeros((3, planes, TILE, nz), jnp.float32)
    if hi == ny:
        for ref, planes in ((start_ref, 6), (step_ref, 4)):
            at = pl.ds((tiles + 2) * TILE, TILE)
            ref[0, :, at, :] = jnp.full((planes, TILE, nz), PLATE_SPEED, jnp.float32)
            ref[1:, :, at, :] = jnp.zeros((2, planes, TILE, nz), jnp.float32)

    row = lax.broadcasted_iota(jnp.int32, (TILE, nz), 0)

    def readers(ref, t):
        def tile(c, plane, step):
            at = pl.ds(pl.multiple_of((t + step) * TILE, TILE), TILE)
            return ref[c, plane, at, :]

        def read(c, plane):
            return tile(c, plane, 0)

        def below(c, plane, u):
            return pltpu.roll(jnp.where(row == TILE - 1, tile(c, plane, -1), u), 1, 0)

        def above(c, plane, u):
            return pltpu.roll(jnp.where(row == 0, tile(c, plane, 1), u), TILE - 1, 0)

        return read, below, above

    def first_step(t):
        read, below, above = readers(start_ref, t)
        for plane in range(4):
            fresh = plane_update(read, below, above, plane + 1)
            for c in range(3):
                step_ref[c, plane, pl.ds(pl.multiple_of(t * TILE, TILE), TILE), :] = fresh[c]

    def second_step(t):
        read, below, above = readers(step_ref, t)
        for plane in range(2):
            fresh = plane_update(read, below, above, plane + 1)
            for c in range(3):
                at = pl.ds(pl.multiple_of((t - 2) * TILE, TILE), TILE)
                new_ref[c, plane, at, :] = fresh[c]

    def both_steps(t, carry):
        first_step(t)
        second_step(t - 1)
        return carry

    done_first, done_second = (1 if lo == 0 else 0), 1
    for segment, last_tile in enumerate(segments):
        for copy in pending.get(segment, []):
            copy.wait()
        end_first = tiles + 1 if hi == ny else tiles + 2
        reach_first = min(last_tile - 1, end_first) if segment < len(segments) - 1 else end_first
        reach_second = min(reach_first - 1, tiles + 1)
        while done_first < reach_first and done_second >= done_first:
            done_first += 1
            first_step(done_first)
        head = done_second
        if done_first == done_second + 1:
            begin = done_first + 1
        else:
            while done_first < min(reach_first, done_second + 1):
                done_first += 1
                first_step(done_first)
            begin = done_first + 1
        if reach_first >= begin:
            lax.fori_loop(begin, reach_first + 1, both_steps, 0)
            done_first = reach_first
            done_second = max(done_second, reach_first - 1)
        if segment == len(segments) - 1:
            while done_second < tiles + 1:
                done_second += 1
                second_step(done_second)
        if done_second > head:
            at, count = (head - 1) * TILE, (done_second - head) * TILE
            copy = pltpu.make_async_copy(
                new_ref.at[:, :, pl.ds(at, count), :],
                out_ref.at[:, :, pl.ds(at + (lo if out_ref.shape[2] == ny else 0), count), :],
                out_sem.at[len(outgoing)],
            )
            copy.start()
            outgoing.append(copy)
    if lo == 0:
        write_back(new_ref, refs[n_in + 2])
    for copy in outgoing:
        copy.wait()


def two_steps(core, own, chip, far, lo, hi, ny, cuts=(), into=None, low=None, whole=True):
    nz = own[0][0].shape[-1]
    ins, copies = [], []
    floor, ceiling = max(lo - TILE, 0), min(hi + TILE, ny)
    edges = [floor] + [cut for cut in cuts if floor < cut < ceiling] + [ceiling]
    for plane, pieces in (("own", own), ("chip", chip), ("far", far)):
        for array, first, *least in pieces:
            last = first + array.shape[2]
            used = False
            for segment, (a, b) in enumerate(zip(edges[:-1], edges[1:])):
                a, b = max(a, first, *least), min(b, last)
                if a < b:
                    copies.append(
                        (segment, len(ins), plane, a - first, a - lo + 2 * TILE, b - a)
                    )
                    used = True
            if used:
                ins.append(array)
    segments = [(edge - lo) // TILE + 1 for edge in edges[1:]]
    low_rows = None
    if low is not None:
        low_rows = len(ins)
        ins.append(low)
    aliases = {}
    if into is not None:
        aliases = {len(ins) + 1: 0}
        ins.append(into)
    copies.sort(key=lambda copy: copy[0])
    span = hi - lo
    anywhere = pl.BlockSpec(memory_space=pltpu.HBM)
    return pl.pallas_call(
        functools.partial(
            two_steps_kernel,
            copies=copies,
            segments=segments,
            lo=lo,
            hi=hi,
            ny=ny,
            n_in=len(ins),
            low_rows=low_rows,
        ),
        in_specs=[pl.BlockSpec(memory_space=pltpu.SMEM)] + [anywhere] * len(ins),
        out_specs=[anywhere] + [pl.BlockSpec(memory_space=pltpu.VMEM)] * (lo == 0),
        out_shape=[
            jax.ShapeDtypeStruct((3, 2, ny if whole else span, nz), jnp.float32),
            jax.ShapeDtypeStruct((nz // CZ, 8, LANES), jnp.float32),
        ][: 1 + (lo == 0)],
        scratch_shapes=[
            pltpu.VMEM((3, 6, span + 4 * TILE, nz), jnp.float32),
            pltpu.VMEM((3, 4, span + 4 * TILE, nz), jnp.float32),
            pltpu.VMEM((3, 2, span, nz), jnp.float32),
            pltpu.SemaphoreType.DMA((len(copies),)),
            pltpu.SemaphoreType.DMA((len(segments) + 1,)),
        ],
        input_output_aliases=aliases,
        compiler_params=pltpu.CompilerParams(vmem_limit_bytes=VMEM_BYTES),
        cost_estimate=pl.CostEstimate(
            flops=span * 10**6, bytes_accessed=span * 60 * 10**3, transcendentals=0
        ),
        name="two_steps",
    )(core, *ins)


def tie(value, *others):
    return lax.optimization_barrier((value,) + others)[0]


def local(field, atom_vel, cell_ids, fluid):
    ny = field.shape[2]
    count = lax.axis_size("gx") * lax.axis_size("gz")
    core = (lax.axis_index("gz") % 2).reshape(1)
    chip_pairs, far_pairs = [], []
    for i in range(0, count, 2):
        chip_pairs += [(i, i + 1), (i + 1, i)]
        far_pairs += [(i + 1, (i + 2) % count), ((i + 2) % count, i + 1)]

    def over_chip(block):
        return lax.ppermute(block, ROW_AXES, chip_pairs)

    def over_links(block):
        return lax.ppermute(block, ROW_AXES, far_pairs)

    def exchange(block):
        return lax.all_to_all(block, "gz", split_axis=0, concat_axis=0, tiled=True)

    first = over_links(field[:, :, LOW:FIRST])
    chip = over_chip(field)
    means, outgoing, *blocks = cell_means(
        atom_vel, cell_ids, fluid, field, (FIRST, SECOND, THIRD, ny)
    )
    slab = exchange(outgoing)
    base = seed(slab, field)
    base_chip, base_far = over_chip(base), over_links(base)
    second = over_links(tie(blocks[0], base_chip, base_far, first, chip))
    low, returned = two_steps(
        core,
        [(base, 0), (field, 0, LOW)],
        [(base_chip, 0), (chip, 0, LOW)],
        [(base_far, 0), (first, LOW)],
        0,
        TILE,
        ny,
        whole=False,
    )
    back = exchange(returned)
    own, beside = [(field, 0)], [(chip, 0)]
    far = [(base_far, 0), (first, LOW), (second, FIRST)]
    start, reach = TILE, FIRST - TILE
    (part,) = two_steps(core, own, beside, far[:2], start, reach, ny, (40, 72))
    third = over_links(tie(blocks[1], second, back, part))
    far.append((third, SECOND))
    new_atoms = constrain(atom_vel, cell_ids, fluid, back, means)
    start, reach = reach, SECOND - TILE
    (part,) = two_steps(core, own, beside, far[1:3], start, reach, ny, (136,), into=part)
    far.append((over_links(tie(blocks[2], part, new_atoms)), THIRD))
    start, reach = reach, THIRD - TILE
    (part,) = two_steps(core, own, beside, far[2:4], start, reach, ny, (192,), into=part)
    (new_field,) = two_steps(
        core, own, beside, far[3:], reach, ny, ny, into=part, low=low
    )
    return new_field, new_atoms


def solution(mesh):
    placed = (
        P(None, ("gx", "gz"), None, None),
        P(None, None, "gx", "gz"),
        P(None, "gx", "gz"),
        P(None, "gx", "gz"),
    )
    return jax.shard_map(
        local,
        mesh=mesh,
        in_specs=placed,
        out_specs=(P(None, ("gx", "gz"), None, None), P(None, None, "gx", "gz")),
        check_vma=False,
    )
```

time: 149 us -> 101 us (0.68)
  waiting for transfers between devices: 65.5 us -> 13.1 us
  blocking collectives: 0 us -> 17.1 us
  local copies, waits for them, and re-layouts: 17.4 us -> 2.51 us
  Pallas kernels: 37.3 us -> 45.3 us
  starting transfers between devices: 27.7 us -> 21.4 us
    ppermute x8 -> x7, waiting for transfers between devices: 57.3 us -> 13.1 us  [the longest x5 13.1 us: over_links(): return lax.ppermute(block, ROW_AXES, far_pairs)]
    all_to_all x0 -> x1, blocking collectives: none -> 17.1 us  [exchange(): return lax.all_to_all(block, 'gz', split_axis=0, concat_axis=0, tiled=True)]
    all_to_all x2 -> x1, waiting for transfers between devices: 8.13 us -> 0.01 us  [exchange(): return lax.all_to_all(block, 'gz', split_axis=0, concat_axis=0, tiled=True)]
    pallas_call x3 -> x5, Pallas kernels: 14.8 us -> 22.7 us  [two_steps(): pl.pallas_call(functools.partial(two_steps_kernel, copies=copies, segment...]
    all_to_all x2 -> x1, starting transfers between devices: 19.7 us -> 13.7 us  [exchange(): return lax.all_to_all(block, 'gz', split_axis=0, concat_axis=0, tiled=True)]
    all_to_all x3 -> x0, local copies, waits for them, and re-layouts: 4.44 us -> none  [the longest x2 3.04 us: local(): back = lax.all_to_all(back, 'gz', split_axis=0, concat_axis=0, tiled=True)]
    unnamed x11 -> x0, local copies, waits for them, and re-layouts: 3.46 us -> none
    reshape x3 -> x0, local copies, waits for them, and re-layouts: 3.21 us -> none  [the longest x2 1.74 us: local(): slab = slab.reshape(blocks, planes, OY, 4, CZ).transpose(3, 1, 2, 0, 4)]
  transfers between devices with their start and end apart: 10 -> 8, of which waited for: 6 -> 3; matrix products, arithmetic and copies ran while one was open for 2% -> 3% of each run, Pallas kernels for 9% -> 41%
where the time goes in v1:
time: 101 us; the launch traced here: 100 us
  Pallas kernels  45.3 us (45%)
  starting transfers between devices  21.4 us (21%)
  blocking collectives  17.1 us (17%)
  waiting for transfers between devices  13.1 us (13%)
  local copies, waits for them, and re-layouts  2.51 us (2%)
    pallas_call x5, Pallas kernels, two_steps(): pl.pallas_call(functools.partial(two_steps_kernel, copies=copies, segment...  22.7 us
    all_to_all x1, blocking collectives, exchange(): return lax.all_to_all(block, 'gz', split_axis=0, concat_axis=0, tiled=True)  17.1 us
    pallas_call x1, Pallas kernels, cell_means(): pl.pallas_call(functools.partial(means_kernel, atoms=atoms, cuts=cuts), g...  15.1 us
    all_to_all x1, starting transfers between devices, exchange(): return lax.all_to_all(block, 'gz', split_axis=0, concat_axis=0, tiled=True)  13.7 us
    ppermute x5, waiting for transfers between devices, over_links(): return lax.ppermute(block, ROW_AXES, far_pairs)  13.1 us
    ppermute x5, starting transfers between devices, over_links(): return lax.ppermute(block, ROW_AXES, far_pairs)  6.77 us
    pallas_call x1, Pallas kernels, constrain(): pl.pallas_call(functools.partial(constrain_kernel, atoms=atoms), grid=(nx...  5.77 us
    slice x1, local copies, waits for them, and re-layouts, local(): first = over_links(field[:, :, LOW:FIRST])  2.51 us
  transfers between devices with their start and end apart: 8, of which 3 were waited for; matrix products, arithmetic and copies ran while one was open for 3% of the time, Pallas kernels for 41%

profile of v1, /device:TPU:3, one launch (start us, length us, event | category | flops | bytes accessed | tf_op | source)
XLA Modules:
  0.0 100.1 jit_solution(12544862972253052968)
XLA Ops:
  0.6 0.8 collective-permute-start
  1.4 2.5 %slice.3 = f32[3,2,104,512]{3,2,1,0:T(8,128)} slice(f32[3,2,256,512]{3,2,1,0:T(8,128)} %refs_1_.7), slice={[0:3], [0:2], [8:112], [0:512]} | slice | bytes 2555904 | tf_op jit(solution)/shard_map/slice | solution.py:456
  3.9 1.2 %collective-permute-start.3 = (f32[3,2,104,512]{3,2,1,0:T(8,128)}, f32[3,2,104,512]{3,2,1,0:T(8,128)}, u32[]{:S(2)}, u32[]{:S(2)}) collective-permute-start(f32[3,2,104,512]{3,2,1,0:T(8,128)} %slice.3), channel_id=1, source_target_pairs={{1,2},{2,1},{3,4},{4,3},{5,6},{6,5},{7,8},{8,7},{9,10},{10,9},{11,... | collective-permute-start | bytes 3833864 | tf_op jit(solution)/shard_map/ppermute | solution.py:451
  5.1 15.1 %cell_means.1 = (f32[32,256]{1,0:T(8,128)}, f32[16,8,128]{2,1,0:T(8,128)}, f32[3,2,56,512]{3,2,1,0:T(8,128)}, f32[3,2,64,512]{3,2,1,0:T(8,128)}, f32[3,2,24,512]{3,2,1,0:T(8,128)}) custom-call(f32[3,2,32,4096]{3,2,1,0:T(8,128)} %vel_ref.3, s32[2,32,4096]{2,1,0:T(8,128)} %ids_ref.3, s32[2,32,4096]{2,1,0:T(8,128)} %fluid_ref.3, f32[3,2,256,512]{3,2,1,0:T(8,128)} %refs_1_.7), custom_call_target="tpu_custom_call" | custom-call | flops 100000000 | bytes 40000000 | tf_op jit(solution)/shard_map/cell_means/pallas_call | solution.py:112
  20.2 17.1 %all_to_all.10.slab_ref = f32[16,8,128]{2,1,0:T(8,128)} all-to-all(f32[16,8,128]{2,1,0:T(8,128)} %get-tuple-element.14), channel_id=1, replica_groups=mesh['gx'=8,'gz'=16] {'gz'}, dimensions={0} | all-to-all | bytes 131072 | tf_op jit(solution)/shard_map/all_to_all | solution.py:454
  37.3 1.7 %seed.1.refs_1_ = f32[3,2,8,512]{3,2,1,0:T(8,128)} custom-call(f32[16,8,128]{2,1,0:T(8,128)} %all_to_all.10.slab_ref, f32[3,2,256,512]{3,2,1,0:T(8,128)} %refs_1_.7), custom_call_target="tpu_custom_call" | custom-call | tf_op jit(solution)/shard_map/seed/pallas_call | solution.py:176
  39.0 1.0 collective-permute-start.2
  40.0 0.2 collective-permute-start.1
  40.2 4.1 %collective-permute-done.2.refs_5_.refs_3_ = f32[3,2,8,512]{3,2,1,0:T(8,128)} collective-permute-done((f32[3,2,8,512]{3,2,1,0:T(8,128)}, f32[3,2,8,512]{3,2,1,0:T(8,128)}, u32[]{:S(2)}, u32[]{:S(2)}) %collective-permute-start.2) | collective-permute-done | bytes 98336 | tf_op jit(solution)/shard_map/ppermute | solution.py:451
  44.2 0.0 collective-permute-done.1.refs_3_
  44.2 0.0 collective-permute-done.3.refs_6_.refs_4_.refs_3_
  44.3 0.0 collective-permute-done.refs_4_.refs_2_
  44.3 1.8 %collective-permute-start.4 = (f32[3,2,56,512]{3,2,1,0:T(8,128)}, f32[3,2,56,512]{3,2,1,0:T(8,128)}, u32[]{:S(2)}, u32[]{:S(2)}) collective-permute-start(f32[3,2,56,512]{3,2,1,0:T(8,128)} %get-tuple-element.15), channel_id=1, source_target_pairs={{1,2},{2,1},{3,4},{4,3},{5,6},{6,5},{7,8},{8,7},{9,10},{10,9},{11,... | collective-permute-start | bytes 2064392 | tf_op jit(solution)/shard_map/ppermute | solution.py:451
  46.1 2.8 %two_steps.5 = (f32[3,2,8,512]{3,2,1,0:T(8,128)}, f32[16,8,128]{2,1,0:T(8,128)}) custom-call(s32[1]{0:T(128)} %bitcast.refs_0_, f32[3,2,8,512]{3,2,1,0:T(8,128)} %seed.1.refs_1_, f32[3,2,256,512]{3,2,1,0:T(8,128)} %refs_1_.7, f32[3,2,8,512]{3,2,1,0:T(8,128)} %collective-permute-done.1.refs_3_, f32[3,2,256,512]{3,2,1,0:T(8,128)} %collective-permute-done.refs_4_.refs_2_, ...), custom_call_target="tpu_custom_call" | custom-call | flops 8000000 | bytes 480000 | tf_op jit(solution)/shard_map/two_steps/pallas_call | solution.py:401
  48.9 13.7 %all-to-all-start.1 = ((f32[16,8,128]{2,1,0:T(8,128)}), f32[16,8,128]{2,1,0:T(8,128)}, u32[]{:S(2)}, u32[]{:S(2)}) async-start(f32[16,8,128]{2,1,0:T(8,128)} %get-tuple-element.16), calls=%async_computation.1 | async-start | bytes 131072 | tf_op jit(solution)/shard_map/all_to_all | solution.py:454
  62.6 6.2 %two_steps.6.refs_5_ = f32[3,2,256,512]{3,2,1,0:T(8,128)} custom-call(s32[1]{0:T(128)} %bitcast.refs_0_, f32[3,2,256,512]{3,2,1,0:T(8,128)} %refs_1_.7, f32[3,2,256,512]{3,2,1,0:T(8,128)} %collective-permute-done.refs_4_.refs_2_, f32[3,2,8,512]{3,2,1,0:T(8,128)} %collective-permute-done.2.refs_5_.refs_3_, ...), custom_call_target="tpu_custom_call" | custom-call | flops 96000000 | bytes 5760000 | tf_op jit(solution)/shard_map/two_steps/pallas_call | solution.py:401
  68.8 0.0 all-to-all-done.1.new_ref
  68.8 0.0 collective-permute-done.4.refs_4_.refs_3_
  68.8 1.5 %collective-permute-start.5 = (f32[3,2,64,512]{3,2,1,0:T(8,128)}, f32[3,2,64,512]{3,2,1,0:T(8,128)}, u32[]{:S(2)}, u32[]{:S(2)}) collective-permute-start(f32[3,2,64,512]{3,2,1,0:T(8,128)} %get-tuple-element.17), channel_id=1, source_target_pairs={{1,2},{2,1},{3,4},{4,3},{5,6},{6,5},{7,8},{8,7},{9,10},{10,9},{11,... | collective-permute-start | bytes 2359304 | tf_op jit(solution)/shard_map/ppermute | solution.py:451
  70.3 5.8 %constrain.1 = f32[3,2,32,4096]{3,2,1,0:T(8,128)} custom-call(f32[3,2,32,4096]{3,2,1,0:T(8,128)} %vel_ref.3, s32[2,32,4096]{2,1,0:T(8,128)} %ids_ref.3, s32[2,32,4096]{2,1,0:T(8,128)} %fluid_ref.3, f32[16,8,128]{2,1,0:T(8,128)} %all-to-all-done.1.new_ref, f32[32,256]{1,0:T(8,128)} %get-tuple-element.19.mean_ref), custom_call_target="tpu_custom_call" | custom-call | flops 10000000 | bytes 20000000 | tf_op jit(solution)/shard_map/constrain/pallas_call | solution.py:224
  76.1 4.6 %two_steps.7.refs_5_ = f32[3,2,256,512]{3,2,1,0:T(8,128)} custom-call(s32[1]{0:T(128)} %bitcast.refs_0_, f32[3,2,256,512]{3,2,1,0:T(8,128)} %refs_1_.7, f32[3,2,256,512]{3,2,1,0:T(8,128)} %collective-permute-done.refs_4_.refs_2_, f32[3,2,104,512]{3,2,1,0:T(8,128)} %collective-permute-done.3.refs_6_.refs_4_.refs_3_, ...), custom_call_target="tpu_custom_call", output_to_operand_aliasing={{}: (5, {})} | custom-call | flops 56000000 | bytes 3360000 | tf_op jit(solution)/shard_map/two_steps/pallas_call | solution.py:401
  80.7 1.3 %collective-permute-start.6 = (f32[3,2,24,512]{3,2,1,0:T(8,128)}, f32[3,2,24,512]{3,2,1,0:T(8,128)}, u32[]{:S(2)}, u32[]{:S(2)}) collective-permute-start(f32[3,2,24,512]{3,2,1,0:T(8,128)} %get-tuple-element.20), channel_id=1, source_target_pairs={{1,2},{2,1},{3,4},{4,3},{5,6},{6,5},{7,8},{8,7},{9,10},{10,9},{11,... | collective-permute-start | bytes 884744 | tf_op jit(solution)/shard_map/ppermute | solution.py:451
  82.0 7.9 %collective-permute-done.5.refs_4_.refs_3_ = f32[3,2,64,512]{3,2,1,0:T(8,128)} collective-permute-done((f32[3,2,64,512]{3,2,1,0:T(8,128)}, f32[3,2,64,512]{3,2,1,0:T(8,128)}, u32[]{:S(2)}, u32[]{:S(2)}) %collective-permute-start.5) | collective-permute-done | bytes 786464 | tf_op jit(solution)/shard_map/ppermute | solution.py:451
  90.0 5.0 %two_steps.8.refs_6_ = f32[3,2,256,512]{3,2,1,0:T(8,128)} custom-call(s32[1]{0:T(128)} %bitcast.refs_0_, f32[3,2,256,512]{3,2,1,0:T(8,128)} %refs_1_.7, f32[3,2,256,512]{3,2,1,0:T(8,128)} %collective-permute-done.refs_4_.refs_2_, f32[3,2,56,512]{3,2,1,0:T(8,128)} %collective-permute-done.4.refs_4_.refs_3_, ...), custom_call_target="tpu_custom_call", output_to_operand_aliasing={{}: (5, {})} | custom-call | flops 64000000 | bytes 3840000 | tf_op jit(solution)/shard_map/two_steps/pallas_call | solution.py:401
  94.9 1.1 %collective-permute-done.6.refs_4_ = f32[3,2,24,512]{3,2,1,0:T(8,128)} collective-permute-done((f32[3,2,24,512]{3,2,1,0:T(8,128)}, f32[3,2,24,512]{3,2,1,0:T(8,128)}, u32[]{:S(2)}, u32[]{:S(2)}) %collective-permute-start.6) | collective-permute-done | bytes 294944 | tf_op jit(solution)/shard_map/ppermute | solution.py:451
  96.0 4.1 %two_steps.9 = f32[3,2,256,512]{3,2,1,0:T(8,128)} custom-call(s32[1]{0:T(128)} %bitcast.refs_0_, f32[3,2,256,512]{3,2,1,0:T(8,128)} %refs_1_.7, f32[3,2,256,512]{3,2,1,0:T(8,128)} %collective-permute-done.refs_4_.refs_2_, f32[3,2,64,512]{3,2,1,0:T(8,128)} %collective-permute-done.5.refs_4_.refs_3_, ...), custom_call_target="tpu_custom_call", output_to_operand_aliasing={{}: (6, {})} | custom-call | flops 32000000 | bytes 1920000 | tf_op jit(solution)/shard_map/two_steps/pallas_call | solution.py:401
Async XLA Ops:
  0.6 43.6 %collective-permute-start = (f32[3,2,256,512]{3,2,1,0:T(8,128)}, f32[3,2,256,512]{3,2,1,0:T(8,128)}, u32[]{:S(2)}, u32[]{:S(2)}) collective-permute-start(f32[3,2,256,512]{3,2,1,0:T(8,128)} %refs_1_.7), channel_id=1, source_target_pairs={{0,1},{1,0},{2,3},{3,2},{4,5},{5,4},{6,7},{7,6},{8,9},{9,8},{10,11... | collective-permute-start | bytes 9437192 | tf_op jit(solution)/shard_map/ppermute | solution.py:448
  3.9 40.4 %collective-permute-start.3 = (f32[3,2,104,512]{3,2,1,0:T(8,128)}, f32[3,2,104,512]{3,2,1,0:T(8,128)}, u32[]{:S(2)}, u32[]{:S(2)}) collective-permute-start(f32[3,2,104,512]{3,2,1,0:T(8,128)} %slice.3), channel_id=1, source_target_pairs={{1,2},{2,1},{3,4},{4,3},{5,6},{6,5},{7,8},{8,7},{9,10},{10,9},{11,... | collective-permute-start | bytes 3833864 | tf_op jit(solution)/shard_map/ppermute | solution.py:451
  39.0 5.3 %collective-permute-start.2 = (f32[3,2,8,512]{3,2,1,0:T(8,128)}, f32[3,2,8,512]{3,2,1,0:T(8,128)}, u32[]{:S(2)}, u32[]{:S(2)}) collective-permute-start(f32[3,2,8,512]{3,2,1,0:T(8,128)} %seed.1.refs_1_), channel_id=1, source_target_pairs={{1,2},{2,1},{3,4},{4,3},{5,6},{6,5},{7,8},{8,7},{9,10},{10,9},{11,... | collective-permute-start | bytes 294920 | tf_op jit(solution)/shard_map/ppermute | solution.py:451
  40.0 4.3 %collective-permute-start.1 = (f32[3,2,8,512]{3,2,1,0:T(8,128)}, f32[3,2,8,512]{3,2,1,0:T(8,128)}, u32[]{:S(2)}, u32[]{:S(2)}) collective-permute-start(f32[3,2,8,512]{3,2,1,0:T(8,128)} %seed.1.refs_1_), channel_id=1, source_target_pairs={{0,1},{1,0},{2,3},{3,2},{4,5},{5,4},{6,7},{7,6},{8,9},{9,8},{10,11... | collective-permute-start | bytes 294920 | tf_op jit(solution)/shard_map/ppermute | solution.py:448
  44.3 24.6 %collective-permute-start.4 = (f32[3,2,56,512]{3,2,1,0:T(8,128)}, f32[3,2,56,512]{3,2,1,0:T(8,128)}, u32[]{:S(2)}, u32[]{:S(2)}) collective-permute-start(f32[3,2,56,512]{3,2,1,0:T(8,128)} %get-tuple-element.15), channel_id=1, source_target_pairs={{1,2},{2,1},{3,4},{4,3},{5,6},{6,5},{7,8},{8,7},{9,10},{10,9},{11,... | collective-permute-start | bytes 2064392 | tf_op jit(solution)/shard_map/ppermute | solution.py:451
  48.9 19.9 %all-to-all-start.1 = ((f32[16,8,128]{2,1,0:T(8,128)}), f32[16,8,128]{2,1,0:T(8,128)}, u32[]{:S(2)}, u32[]{:S(2)}) async-start(f32[16,8,128]{2,1,0:T(8,128)} %get-tuple-element.16), calls=%async_computation.1 | async-start | bytes 131072 | tf_op jit(solution)/shard_map/all_to_all | solution.py:454
  68.8 21.1 %collective-permute-start.5 = (f32[3,2,64,512]{3,2,1,0:T(8,128)}, f32[3,2,64,512]{3,2,1,0:T(8,128)}, u32[]{:S(2)}, u32[]{:S(2)}) collective-permute-start(f32[3,2,64,512]{3,2,1,0:T(8,128)} %get-tuple-element.17), channel_id=1, source_target_pairs={{1,2},{2,1},{3,4},{4,3},{5,6},{6,5},{7,8},{8,7},{9,10},{10,9},{11,... | collective-permute-start | bytes 2359304 | tf_op jit(solution)/shard_map/ppermute | solution.py:451
  80.7 15.2 %collective-permute-start.6 = (f32[3,2,24,512]{3,2,1,0:T(8,128)}, f32[3,2,24,512]{3,2,1,0:T(8,128)}, u32[]{:S(2)}, u32[]{:S(2)}) collective-permute-start(f32[3,2,24,512]{3,2,1,0:T(8,128)} %get-tuple-element.20), channel_id=1, source_target_pairs={{1,2},{2,1},{3,4},{4,3},{5,6},{6,5},{7,8},{8,7},{9,10},{10,9},{11,... | collective-permute-start | bytes 884744 | tf_op jit(solution)/shard_map/ppermute | solution.py:451

commit v2 on v1

--- a/solution.py
+++ b/solution.py
@@ -11,12 +11,11 @@
 OY = 2
 LANES = 128
 TILE = 8
-GROUP = 16
+CHUNK = 2048
 VMEM_BYTES = 64 * 2**20
 LOW = 8
-FIRST = 112
-SECOND = 168
-THIRD = 232
+FIRST = 104
+SECOND = 184
 
 VISCOUS = 0.15
 COURANT = 0.05
@@ -25,8 +24,22 @@
 ROW_AXES = ("gx", "gz")
 
 
+def product(a, b, contract):
+    return lax.dot_general(
+        a, b, (((1,), (contract,)), ((), ())), preferred_element_type=jnp.float32
+    )
+
+
+def in_bfloat16(values):
+    terms = []
+    for _ in range(3):
+        terms.append(values.astype(jnp.bfloat16).astype(jnp.float32))
+        values = values - terms[-1]
+    return terms
+
+
 def means_kernel(vel_ref, ids_ref, fluid_ref, field_ref, out_ref, send_ref, *refs, atoms, cuts):
-    pieces, (key_ref, one_ref, held_ref, sem) = refs[:-4], refs[-4:]
+    pieces, (held_ref, sem) = refs[:-2], refs[-2:]
     fetch = pltpu.make_async_copy(
         field_ref.at[:, :, pl.ds(cuts[0], cuts[-1] - cuts[0]), :], held_ref, sem.at[len(pieces)]
     )
@@ -47,53 +60,42 @@
         for copy in copies:
             copy.start()
 
-    columns = atoms // LANES
-    lane = lax.broadcasted_iota(jnp.int32, (TILE, LANES), 1)
-
-    def window(j):
-        return pl.ds(pl.multiple_of(j * LANES, LANES), LANES)
+    width = CZ * TILE
+    column = lax.broadcasted_iota(jnp.int32, (TILE, width), 1) % TILE
+    agree = column == lax.broadcasted_iota(jnp.int32, (TILE, width), 0)
+    place = lax.broadcasted_iota(jnp.int32, (width, LANES), 0) // TILE
+    gather = place == lax.broadcasted_iota(jnp.int32, (width, LANES), 1)
+    gather = jnp.where(gather, 1.0, 0.0).astype(jnp.bfloat16)
+    upper = lax.broadcasted_iota(jnp.int32, (2 * TILE, CHUNK), 0) // TILE
+    upper = upper.astype(jnp.float32)
+    one = jnp.ones((2 * TILE, CHUNK), jnp.bfloat16)
+    nil = jnp.zeros((2 * TILE, CHUNK), jnp.bfloat16)
 
     for r in range(OY):
 
-        def prepare(j, carry):
-            at = window(j)
-            cell = jnp.where(fluid_ref[r, :, at] > 0, ids_ref[r, :, at], -1)
-            key_ref[:, at] = cell
-            one_ref[:, at] = lax.shift_left(jnp.int32(1), (cell & 3) * 8)
-            return carry
-
-        lax.fori_loop(0, columns, prepare, 0, unroll=8)
-        out = jnp.zeros((TILE, LANES), jnp.float32)
-        for first in range(0, CZ, GROUP):
-
-            def body(j, totals):
-                at = window(j)
-                cell, one = key_ref[:, at], one_ref[:, at]
-                v = [vel_ref[c, r, :, at] for c in range(3)]
-                totals = list(totals)
-                for k in range(GROUP):
-                    hit = cell == first + k
-                    for c in range(3):
-                        totals[3 * k + c] = totals[3 * k + c] + jnp.where(hit, v[c], 0.0)
-                quad = lax.shift_right_arithmetic(cell, 2)
-                for q in range(GROUP // 4):
-                    totals[3 * GROUP + q] = totals[3 * GROUP + q] + jnp.where(
-                        quad == first // 4 + q, one, 0
-                    )
-                return tuple(totals)
-
-            zero = [jnp.zeros((TILE, LANES), jnp.float32)] * (3 * GROUP)
-            zero += [jnp.zeros((TILE, LANES), jnp.int32)] * (GROUP // 4)
-            totals = lax.fori_loop(0, columns, body, tuple(zero), unroll=4)
-            for k in range(GROUP):
-                packed = totals[3 * GROUP + k // 4]
-                count = lax.shift_right_logical(packed, (k % 4) * 8) & 255
-                count = jnp.sum(count.astype(jnp.float32), axis=1, keepdims=True)
-                divisor = jnp.maximum(count, 1.0)
-                for c in range(3):
-                    total = jnp.sum(totals[3 * k + c], axis=1, keepdims=True)
-                    out = jnp.where(lane == c * CZ + first + k, total / divisor, out)
-                out = jnp.where(lane == 3 * CZ + first + k, count, out)
+        def body(j, total):
+            at = pl.ds(pl.multiple_of(j * CHUNK, CHUNK), CHUNK)
+            cell = jnp.where(fluid_ref[r, :, at] > 0, ids_ref[r, :, at], -1).astype(jnp.float32)
+            cell = (jnp.concatenate([cell, cell], 0) - upper).astype(jnp.bfloat16)
+            hits = [jnp.where(cell == jnp.bfloat16(k), one, nil) for k in range(0, CZ, 2)]
+            terms = in_bfloat16(jnp.concatenate([vel_ref[c, r, :, at] for c in range(3)], 0))
+            terms.append(jnp.ones((TILE, CHUNK), jnp.float32))
+            terms = jnp.concatenate(terms, 0).astype(jnp.bfloat16)
+            return total + product(terms, jnp.concatenate(hits, 0), 1)
+
+        total = jnp.zeros((10 * TILE, width), jnp.float32)
+        total = lax.fori_loop(0, atoms // CHUNK, body, total)
+        sums = total[: 3 * TILE] + total[3 * TILE : 6 * TILE] + total[6 * TILE : 9 * TILE]
+        parts = [sums[c * TILE : (c + 1) * TILE] for c in range(3)] + [total[9 * TILE :]]
+        parts = jnp.concatenate([jnp.where(agree, part, 0.0) for part in parts], 0)
+        found = product(jnp.concatenate(in_bfloat16(parts), 0).astype(jnp.bfloat16), gather, 0)
+        found = found[: 4 * TILE] + found[4 * TILE : 8 * TILE] + found[8 * TILE :]
+        count = found[3 * TILE :]
+        divisor = jnp.maximum(count, 1.0)
+        out = pltpu.roll(count, 3 * CZ, 1)
+        for c in range(3):
+            mean = found[c * TILE : (c + 1) * TILE] / divisor
+            out = out + (pltpu.roll(mean, c * CZ, 1) if c else mean)
         out_ref[:, pl.ds(r * LANES, LANES)] = out
         for x in range(TILE):
             send_ref[x // 2, pl.ds((x % 2) * OY + r, 1), :] = out[x : x + 1]
@@ -107,7 +109,7 @@
 
 def cell_means(vel, ids, fluid, field, cuts):
     _, _, nx, atoms = vel.shape
-    assert atoms // LANES < 256 and nx >= 2 * TILE
+    assert nx >= 2 * TILE and atoms % CHUNK == 0
     atom_block = pl.BlockSpec((OY, TILE, atoms), lambda x: (0, x, 0))
     return pl.pallas_call(
         functools.partial(means_kernel, atoms=atoms, cuts=cuts),
@@ -131,8 +133,7 @@
             jax.ShapeDtypeStruct((3, 2, b - a, field.shape[3]), jnp.float32)
             for a, b in zip(cuts[:-1], cuts[1:])
         ],
-        scratch_shapes=[pltpu.VMEM((TILE, atoms), jnp.int32)] * 2
-        + [
+        scratch_shapes=[
             pltpu.VMEM((3, 2, cuts[-1] - cuts[0], field.shape[3]), jnp.float32),
             pltpu.SemaphoreType.DMA((len(cuts),)),
         ],
@@ -456,7 +457,7 @@
     first = over_links(field[:, :, LOW:FIRST])
     chip = over_chip(field)
     means, outgoing, *blocks = cell_means(
-        atom_vel, cell_ids, fluid, field, (FIRST, SECOND, THIRD, ny)
+        atom_vel, cell_ids, fluid, field, (FIRST, SECOND, ny)
     )
     slab = exchange(outgoing)
     base = seed(slab, field)
@@ -475,18 +476,13 @@
     back = exchange(returned)
     own, beside = [(field, 0)], [(chip, 0)]
     far = [(base_far, 0), (first, LOW), (second, FIRST)]
-    start, reach = TILE, FIRST - TILE
-    (part,) = two_steps(core, own, beside, far[:2], start, reach, ny, (40, 72))
-    third = over_links(tie(blocks[1], second, back, part))
+    third = over_links(tie(blocks[1], second, back))
     far.append((third, SECOND))
     new_atoms = constrain(atom_vel, cell_ids, fluid, back, means)
-    start, reach = reach, SECOND - TILE
-    (part,) = two_steps(core, own, beside, far[1:3], start, reach, ny, (136,), into=part)
-    far.append((over_links(tie(blocks[2], part, new_atoms)), THIRD))
-    start, reach = reach, THIRD - TILE
-    (part,) = two_steps(core, own, beside, far[2:4], start, reach, ny, (192,), into=part)
+    start, reach = TILE, SECOND - TILE
+    (part,) = two_steps(core, own, beside, far[:3], start, reach, ny, (40, 72, 104, 136))
     (new_field,) = two_steps(
-        core, own, beside, far[3:], reach, ny, ny, into=part, low=low
+        core, own, beside, far[2:], reach, ny, ny, (208, 232), into=part, low=low
     )
     return new_field, new_atoms
 

time: 101 us -> 96.1 us (0.951)
  blocking collectives: 17.1 us -> 39.9 us
  starting transfers between devices: 21.4 us -> 6.71 us
  Pallas kernels: 45.3 us -> 35.8 us
  waiting for transfers between devices: 13.1 us -> 9.55 us
    all_to_all x1 -> x2, blocking collectives: 17.1 us -> 39.9 us  [exchange(): return lax.all_to_all(block, 'gz', split_axis=0, concat_axis=0, tiled=True)]
    all_to_all x1 -> x0, starting transfers between devices: 13.7 us -> none  [exchange(): return lax.all_to_all(block, 'gz', split_axis=0, concat_axis=0, tiled=True)]
    pallas_call x5 -> x3, Pallas kernels: 22.7 us -> 17.2 us  [two_steps(): pl.pallas_call(functools.partial(two_steps_kernel, copies=copies, segment...]
    pallas_call x1, Pallas kernels: 15.1 us -> 11.1 us  [cell_means(): pl.pallas_call(functools.partial(means_kernel, atoms=atoms, cuts=cuts), g...]
    ppermute x5 -> x4, waiting for transfers between devices: 13.1 us -> 9.54 us  [over_links(): return lax.ppermute(block, ROW_AXES, far_pairs)]
    ppermute x5 -> x4, starting transfers between devices: 6.77 us -> 5.72 us  [over_links(): return lax.ppermute(block, ROW_AXES, far_pairs)]
  transfers between devices with their start and end apart: 8 -> 6, of which waited for: 3 -> 2; matrix products, arithmetic and copies ran while one was open for 3% -> 3% of each run, Pallas kernels for 41% -> 32%
where the time goes in v2:
time: 96.1 us; the launch traced here: 95 us
  blocking collectives  39.9 us (42%)
  Pallas kernels  35.8 us (37%)
  waiting for transfers between devices  9.55 us (10%)
  starting transfers between devices  6.71 us (7%)
  local copies, waits for them, and re-layouts  2.42 us (3%)
    all_to_all x2, blocking collectives, exchange(): return lax.all_to_all(block, 'gz', split_axis=0, concat_axis=0, tiled=True)  39.9 us
    pallas_call x3, Pallas kernels, two_steps(): pl.pallas_call(functools.partial(two_steps_kernel, copies=copies, segment...  17.2 us
    pallas_call x1, Pallas kernels, cell_means(): pl.pallas_call(functools.partial(means_kernel, atoms=atoms, cuts=cuts), g...  11.1 us
    ppermute x4, waiting for transfers between devices, over_links(): return lax.ppermute(block, ROW_AXES, far_pairs)  9.54 us
    pallas_call x1, Pallas kernels, constrain(): pl.pallas_call(functools.partial(constrain_kernel, atoms=atoms), grid=(nx...  5.77 us
    ppermute x4, starting transfers between devices, over_links(): return lax.ppermute(block, ROW_AXES, far_pairs)  5.72 us
    slice x1, local copies, waits for them, and re-layouts, local(): first = over_links(field[:, :, LOW:FIRST])  2.42 us
  transfers between devices with their start and end apart: 6, of which 2 were waited for; matrix products, arithmetic and copies ran while one was open for 3% of the time, Pallas kernels for 32%

profile of v2, /device:TPU:3, one launch (start us, length us, event | category | flops | bytes accessed | tf_op | source)
XLA Modules:
  0.0 95.0 jit_solution(13156200887022366864)
XLA Ops:
  0.6 0.8 collective-permute-start
  1.4 2.4 %slice.3 = f32[3,2,96,512]{3,2,1,0:T(8,128)} slice(f32[3,2,256,512]{3,2,1,0:T(8,128)} %refs_1_.3), slice={[0:3], [0:2], [8:104], [0:512]} | slice | bytes 2359296 | tf_op jit(solution)/shard_map/slice | solution.py:457
  3.8 1.2 %collective-permute-start.3 = (f32[3,2,96,512]{3,2,1,0:T(8,128)}, f32[3,2,96,512]{3,2,1,0:T(8,128)}, u32[]{:S(2)}, u32[]{:S(2)}) collective-permute-start(f32[3,2,96,512]{3,2,1,0:T(8,128)} %slice.3), channel_id=1, source_target_pairs={{1,2},{2,1},{3,4},{4,3},{5,6},{6,5},{7,8},{8,7},{9,10},{10,9},{11,... | collective-permute-start | bytes 3538952 | tf_op jit(solution)/shard_map/ppermute | solution.py:452
  5.0 11.1 %cell_means.1 = (f32[32,256]{1,0:T(8,128)}, f32[16,8,128]{2,1,0:T(8,128)}, f32[3,2,80,512]{3,2,1,0:T(8,128)}, f32[3,2,72,512]{3,2,1,0:T(8,128)}) custom-call(f32[3,2,32,4096]{3,2,1,0:T(8,128)} %vel_ref.3, s32[2,32,4096]{2,1,0:T(8,128)} %ids_ref.3, s32[2,32,4096]{2,1,0:T(8,128)} %fluid_ref.3, f32[3,2,256,512]{3,2,1,0:T(8,128)} %refs_1_.3), custom_call_target="tpu_custom_call" | custom-call | flops 100000000 | bytes 40000000 | tf_op jit(solution)/shard_map/cell_means/pallas_call | solution.py:114
  16.1 19.0 %all_to_all.10.slab_ref = f32[16,8,128]{2,1,0:T(8,128)} all-to-all(f32[16,8,128]{2,1,0:T(8,128)} %get-tuple-element.11), channel_id=1, replica_groups=mesh['gx'=8,'gz'=16] {'gz'}, dimensions={0} | all-to-all | bytes 131072 | tf_op jit(solution)/shard_map/all_to_all | solution.py:455
  35.1 1.7 %seed.1.refs_1_ = f32[3,2,8,512]{3,2,1,0:T(8,128)} custom-call(f32[16,8,128]{2,1,0:T(8,128)} %all_to_all.10.slab_ref, f32[3,2,256,512]{3,2,1,0:T(8,128)} %refs_1_.3), custom_call_target="tpu_custom_call" | custom-call | tf_op jit(solution)/shard_map/seed/pallas_call | solution.py:177
  36.8 0.7 collective-permute-start.2
  37.5 0.2 collective-permute-start.1
  37.8 4.3 %collective-permute-done.2.refs_5_.refs_3_ = f32[3,2,8,512]{3,2,1,0:T(8,128)} collective-permute-done((f32[3,2,8,512]{3,2,1,0:T(8,128)}, f32[3,2,8,512]{3,2,1,0:T(8,128)}, u32[]{:S(2)}, u32[]{:S(2)}) %collective-permute-start.2) | collective-permute-done | bytes 98336 | tf_op jit(solution)/shard_map/ppermute | solution.py:452
  42.0 0.0 collective-permute-done.1.refs_3_
  42.0 0.0 collective-permute-done.3.refs_6_.refs_4_
  42.1 0.0 collective-permute-done.refs_4_.refs_2_
  42.1 1.5 %collective-permute-start.4 = (f32[3,2,80,512]{3,2,1,0:T(8,128)}, f32[3,2,80,512]{3,2,1,0:T(8,128)}, u32[]{:S(2)}, u32[]{:S(2)}) collective-permute-start(f32[3,2,80,512]{3,2,1,0:T(8,128)} %get-tuple-element.12), channel_id=1, source_target_pairs={{1,2},{2,1},{3,4},{4,3},{5,6},{6,5},{7,8},{8,7},{9,10},{10,9},{11,... | collective-permute-start | bytes 2949128 | tf_op jit(solution)/shard_map/ppermute | solution.py:452
  43.6 2.8 %two_steps.3 = (f32[3,2,8,512]{3,2,1,0:T(8,128)}, f32[16,8,128]{2,1,0:T(8,128)}) custom-call(s32[1]{0:T(128)} %bitcast.refs_0_, f32[3,2,8,512]{3,2,1,0:T(8,128)} %seed.1.refs_1_, f32[3,2,256,512]{3,2,1,0:T(8,128)} %refs_1_.3, f32[3,2,8,512]{3,2,1,0:T(8,128)} %collective-permute-done.1.refs_3_, f32[3,2,256,512]{3,2,1,0:T(8,128)} %collective-permute-done.refs_4_.refs_2_, ...), custom_call_target="tpu_custom_call" | custom-call | flops 8000000 | bytes 480000 | tf_op jit(solution)/shard_map/two_steps/pallas_call | solution.py:402
  46.4 20.9 %all_to_all.11.new_ref = f32[16,8,128]{2,1,0:T(8,128)} all-to-all(f32[16,8,128]{2,1,0:T(8,128)} %get-tuple-element.14), channel_id=1, replica_groups=mesh['gx'=8,'gz'=16] {'gz'}, dimensions={0} | all-to-all | bytes 131072 | tf_op jit(solution)/shard_map/all_to_all | solution.py:455
  67.3 0.0 collective-permute-done.4.refs_5_.refs_3_
  67.3 2.3 %collective-permute-start.5 = (f32[3,2,72,512]{3,2,1,0:T(8,128)}, f32[3,2,72,512]{3,2,1,0:T(8,128)}, u32[]{:S(2)}, u32[]{:S(2)}) collective-permute-start(f32[3,2,72,512]{3,2,1,0:T(8,128)} %get-tuple-element.15), channel_id=1, source_target_pairs={{1,2},{2,1},{3,4},{4,3},{5,6},{6,5},{7,8},{8,7},{9,10},{10,9},{11,... | collective-permute-start | bytes 2654216 | tf_op jit(solution)/shard_map/ppermute | solution.py:452
  69.6 5.8 %constrain.1 = f32[3,2,32,4096]{3,2,1,0:T(8,128)} custom-call(f32[3,2,32,4096]{3,2,1,0:T(8,128)} %vel_ref.3, s32[2,32,4096]{2,1,0:T(8,128)} %ids_ref.3, s32[2,32,4096]{2,1,0:T(8,128)} %fluid_ref.3, f32[16,8,128]{2,1,0:T(8,128)} %all_to_all.11.new_ref, f32[32,256]{1,0:T(8,128)} %get-tuple-element.17.mean_ref), custom_call_target="tpu_custom_call" | custom-call | flops 10000000 | bytes 20000000 | tf_op jit(solution)/shard_map/constrain/pallas_call | solution.py:225
  75.3 9.0 %two_steps.4.refs_6_ = f32[3,2,256,512]{3,2,1,0:T(8,128)} custom-call(s32[1]{0:T(128)} %bitcast.refs_0_, f32[3,2,256,512]{3,2,1,0:T(8,128)} %refs_1_.3, f32[3,2,256,512]{3,2,1,0:T(8,128)} %collective-permute-done.refs_4_.refs_2_, f32[3,2,8,512]{3,2,1,0:T(8,128)} %collective-permute-done.2.refs_5_.refs_3_, ...), custom_call_target="tpu_custom_call" | custom-call | flops 168000000 | bytes 10080000 | tf_op jit(solution)/shard_map/two_steps/pallas_call | solution.py:402
  84.3 5.2 %collective-permute-done.5.refs_4_ = f32[3,2,72,512]{3,2,1,0:T(8,128)} collective-permute-done((f32[3,2,72,512]{3,2,1,0:T(8,128)}, f32[3,2,72,512]{3,2,1,0:T(8,128)}, u32[]{:S(2)}, u32[]{:S(2)}) %collective-permute-start.5) | collective-permute-done | bytes 884768 | tf_op jit(solution)/shard_map/ppermute | solution.py:452
  89.6 5.4 %two_steps.5 = f32[3,2,256,512]{3,2,1,0:T(8,128)} custom-call(s32[1]{0:T(128)} %bitcast.refs_0_, f32[3,2,256,512]{3,2,1,0:T(8,128)} %refs_1_.3, f32[3,2,256,512]{3,2,1,0:T(8,128)} %collective-permute-done.refs_4_.refs_2_, f32[3,2,80,512]{3,2,1,0:T(8,128)} %collective-permute-done.4.refs_5_.refs_3_, ...), custom_call_target="tpu_custom_call", output_to_operand_aliasing={{}: (6, {})} | custom-call | flops 80000000 | bytes 4800000 | tf_op jit(solution)/shard_map/two_steps/pallas_call | solution.py:402
Async XLA Ops:
  0.6 41.4 %collective-permute-start = (f32[3,2,256,512]{3,2,1,0:T(8,128)}, f32[3,2,256,512]{3,2,1,0:T(8,128)}, u32[]{:S(2)}, u32[]{:S(2)}) collective-permute-start(f32[3,2,256,512]{3,2,1,0:T(8,128)} %refs_1_.3), channel_id=1, source_target_pairs={{0,1},{1,0},{2,3},{3,2},{4,5},{5,4},{6,7},{7,6},{8,9},{9,8},{10,11... | collective-permute-start | bytes 9437192 | tf_op jit(solution)/shard_map/ppermute | solution.py:449
  3.8 38.2 %collective-permute-start.3 = (f32[3,2,96,512]{3,2,1,0:T(8,128)}, f32[3,2,96,512]{3,2,1,0:T(8,128)}, u32[]{:S(2)}, u32[]{:S(2)}) collective-permute-start(f32[3,2,96,512]{3,2,1,0:T(8,128)} %slice.3), channel_id=1, source_target_pairs={{1,2},{2,1},{3,4},{4,3},{5,6},{6,5},{7,8},{8,7},{9,10},{10,9},{11,... | collective-permute-start | bytes 3538952 | tf_op jit(solution)/shard_map/ppermute | solution.py:452
  36.8 5.3 %collective-permute-start.2 = (f32[3,2,8,512]{3,2,1,0:T(8,128)}, f32[3,2,8,512]{3,2,1,0:T(8,128)}, u32[]{:S(2)}, u32[]{:S(2)}) collective-permute-start(f32[3,2,8,512]{3,2,1,0:T(8,128)} %seed.1.refs_1_), channel_id=1, source_target_pairs={{1,2},{2,1},{3,4},{4,3},{5,6},{6,5},{7,8},{8,7},{9,10},{10,9},{11,... | collective-permute-start | bytes 294920 | tf_op jit(solution)/shard_map/ppermute | solution.py:452
  37.5 4.5 %collective-permute-start.1 = (f32[3,2,8,512]{3,2,1,0:T(8,128)}, f32[3,2,8,512]{3,2,1,0:T(8,128)}, u32[]{:S(2)}, u32[]{:S(2)}) collective-permute-start(f32[3,2,8,512]{3,2,1,0:T(8,128)} %seed.1.refs_1_), channel_id=1, source_target_pairs={{0,1},{1,0},{2,3},{3,2},{4,5},{5,4},{6,7},{7,6},{8,9},{9,8},{10,11... | collective-permute-start | bytes 294920 | tf_op jit(solution)/shard_map/ppermute | solution.py:449
  42.1 25.2 %collective-permute-start.4 = (f32[3,2,80,512]{3,2,1,0:T(8,128)}, f32[3,2,80,512]{3,2,1,0:T(8,128)}, u32[]{:S(2)}, u32[]{:S(2)}) collective-permute-start(f32[3,2,80,512]{3,2,1,0:T(8,128)} %get-tuple-element.12), channel_id=1, source_target_pairs={{1,2},{2,1},{3,4},{4,3},{5,6},{6,5},{7,8},{8,7},{9,10},{10,9},{11,... | collective-permute-start | bytes 2949128 | tf_op jit(solution)/shard_map/ppermute | solution.py:452
  67.3 22.3 %collective-permute-start.5 = (f32[3,2,72,512]{3,2,1,0:T(8,128)}, f32[3,2,72,512]{3,2,1,0:T(8,128)}, u32[]{:S(2)}, u32[]{:S(2)}) collective-permute-start(f32[3,2,72,512]{3,2,1,0:T(8,128)} %get-tuple-element.15), channel_id=1, source_target_pairs={{1,2},{2,1},{3,4},{4,3},{5,6},{6,5},{7,8},{8,7},{9,10},{10,9},{11,... | collective-permute-start | bytes 2654216 | tf_op jit(solution)/shard_map/ppermute | solution.py:452

commit v3 on v2

--- a/solution.py
+++ b/solution.py
@@ -99,7 +99,6 @@
         out_ref[:, pl.ds(r * LANES, LANES)] = out
         for x in range(TILE):
             send_ref[x // 2, pl.ds((x % 2) * OY + r, 1), :] = out[x : x + 1]
-            send_ref[x // 2, pl.ds(4 + (x % 2) * OY + r, 1), :] = out[x : x + 1]
 
     @pl.when(pl.program_id(0) == pl.num_programs(0) - 1)
     def _():
@@ -122,12 +121,12 @@
         ],
         out_specs=[
             pl.BlockSpec((TILE, OY * LANES), lambda x: (x, 0)),
-            pl.BlockSpec((TILE // 2, 8, LANES), lambda x: (x, 0, 0)),
+            pl.BlockSpec((TILE // 2, 2 * OY, LANES), lambda x: (x, 0, 0)),
         ]
         + [pl.BlockSpec(memory_space=pltpu.HBM)] * (len(cuts) - 1),
         out_shape=[
             jax.ShapeDtypeStruct((nx, OY * LANES), jnp.float32),
-            jax.ShapeDtypeStruct((nx // 2, 8, LANES), jnp.float32),
+            jax.ShapeDtypeStruct((nx // 2, 2 * OY, LANES), jnp.float32),
         ]
         + [
             jax.ShapeDtypeStruct((3, 2, b - a, field.shape[3]), jnp.float32)
@@ -202,7 +201,6 @@
                 for p in range(2):
                     line = block[2 * m + p : 2 * m + p + 1]
                     out_ref[4 * q + m, pl.ds(p * OY + r, 1), :] = line
-                    out_ref[4 * q + m, pl.ds(4 + p * OY + r, 1), :] = line
 
 
 def constrain_kernel(vel_ref, ids_ref, fluid_ref, new_ref, mean_ref, out_ref, *, atoms):
@@ -229,7 +227,7 @@
             vel_block,
             atom_block,
             atom_block,
-            pl.BlockSpec((TILE // 2, 8, LANES), lambda x: (x, 0, 0)),
+            pl.BlockSpec((TILE // 2, 2 * OY, LANES), lambda x: (x, 0, 0)),
             pl.BlockSpec((TILE, OY * LANES), lambda x: (x, 0)),
         ],
         out_specs=vel_block,
@@ -414,7 +412,7 @@
         out_specs=[anywhere] + [pl.BlockSpec(memory_space=pltpu.VMEM)] * (lo == 0),
         out_shape=[
             jax.ShapeDtypeStruct((3, 2, ny if whole else span, nz), jnp.float32),
-            jax.ShapeDtypeStruct((nz // CZ, 8, LANES), jnp.float32),
+            jax.ShapeDtypeStruct((nz // CZ, 2 * OY, LANES), jnp.float32),
         ][: 1 + (lo == 0)],
         scratch_shapes=[
             pltpu.VMEM((3, 6, span + 4 * TILE, nz), jnp.float32),

time: 96.1 us -> 95.5 us (level)
  no operation moved by 1% of the time
where the time goes in v3:
time: 95.5 us; the launch traced here: 94.5 us
  blocking collectives  39.7 us (42%)
  Pallas kernels  35.7 us (37%)
  waiting for transfers between devices  9.8 us (10%)
  starting transfers between devices  6.19 us (6%)
  local copies, waits for them, and re-layouts  2.42 us (3%)
    all_to_all x2, blocking collectives, exchange(): return lax.all_to_all(block, 'gz', split_axis=0, concat_axis=0, tiled=True)  39.7 us
    pallas_call x3, Pallas kernels, two_steps(): pl.pallas_call(functools.partial(two_steps_kernel, copies=copies, segment...  17.2 us
    pallas_call x1, Pallas kernels, cell_means(): pl.pallas_call(functools.partial(means_kernel, atoms=atoms, cuts=cuts), g...  11.1 us
    ppermute x4, waiting for transfers between devices, over_links(): return lax.ppermute(block, ROW_AXES, far_pairs)  9.8 us
    pallas_call x1, Pallas kernels, constrain(): pl.pallas_call(functools.partial(constrain_kernel, atoms=atoms), grid=(nx...  5.76 us
    ppermute x4, starting transfers between devices, over_links(): return lax.ppermute(block, ROW_AXES, far_pairs)  5.04 us
    slice x1, local copies, waits for them, and re-layouts, local(): first = over_links(field[:, :, LOW:FIRST])  2.42 us
  transfers between devices with their start and end apart: 6, of which 2 were waited for; matrix products, arithmetic and copies ran while one was open for 3% of the time, Pallas kernels for 32%

profile of v3, /device:TPU:3, one launch (start us, length us, event | category | flops | bytes accessed | tf_op | source)
XLA Modules:
  0.0 94.5 jit_solution(10975764580404140636)
XLA Ops:
  0.6 0.8 collective-permute-start
  1.4 2.4 %slice.3 = f32[3,2,96,512]{3,2,1,0:T(8,128)} slice(f32[3,2,256,512]{3,2,1,0:T(8,128)} %refs_1_.3), slice={[0:3], [0:2], [8:104], [0:512]} | slice | bytes 2359296 | tf_op jit(solution)/shard_map/slice | solution.py:455
  3.8 1.2 %collective-permute-start.3 = (f32[3,2,96,512]{3,2,1,0:T(8,128)}, f32[3,2,96,512]{3,2,1,0:T(8,128)}, u32[]{:S(2)}, u32[]{:S(2)}) collective-permute-start(f32[3,2,96,512]{3,2,1,0:T(8,128)} %slice.3), channel_id=1, source_target_pairs={{1,2},{2,1},{3,4},{4,3},{5,6},{6,5},{7,8},{8,7},{9,10},{10,9},{11,... | collective-permute-start | bytes 3538952 | tf_op jit(solution)/shard_map/ppermute | solution.py:450
  5.0 11.1 %cell_means.1 = (f32[32,256]{1,0:T(8,128)}, f32[16,4,128]{2,1,0:T(4,128)}, f32[3,2,80,512]{3,2,1,0:T(8,128)}, f32[3,2,72,512]{3,2,1,0:T(8,128)}) custom-call(f32[3,2,32,4096]{3,2,1,0:T(8,128)} %vel_ref.3, s32[2,32,4096]{2,1,0:T(8,128)} %ids_ref.3, s32[2,32,4096]{2,1,0:T(8,128)} %fluid_ref.3, f32[3,2,256,512]{3,2,1,0:T(8,128)} %refs_1_.3), custom_call_target="tpu_custom_call" | custom-call | flops 100000000 | bytes 40000000 | tf_op jit(solution)/shard_map/cell_means/pallas_call | solution.py:113
  16.1 18.8 %all_to_all.10.slab_ref = f32[16,4,128]{2,1,0:T(4,128)} all-to-all(f32[16,4,128]{2,1,0:T(4,128)} %get-tuple-element.11), channel_id=1, replica_groups=mesh['gx'=8,'gz'=16] {'gz'}, dimensions={0} | all-to-all | bytes 65536 | tf_op jit(solution)/shard_map/all_to_all | solution.py:453
  34.9 1.7 %seed.1.refs_1_ = f32[3,2,8,512]{3,2,1,0:T(8,128)} custom-call(f32[16,4,128]{2,1,0:T(4,128)} %all_to_all.10.slab_ref, f32[3,2,256,512]{3,2,1,0:T(8,128)} %refs_1_.3), custom_call_target="tpu_custom_call" | custom-call | tf_op jit(solution)/shard_map/seed/pallas_call | solution.py:176
  36.6 0.7 collective-permute-start.2
  37.2 0.4 collective-permute-start.1
  37.6 4.2 %collective-permute-done.2.refs_5_.refs_3_ = f32[3,2,8,512]{3,2,1,0:T(8,128)} collective-permute-done((f32[3,2,8,512]{3,2,1,0:T(8,128)}, f32[3,2,8,512]{3,2,1,0:T(8,128)}, u32[]{:S(2)}, u32[]{:S(2)}) %collective-permute-start.2) | collective-permute-done | bytes 98336 | tf_op jit(solution)/shard_map/ppermute | solution.py:450
  41.8 0.0 collective-permute-done.1.refs_3_
  41.8 0.0 collective-permute-done.3.refs_6_.refs_4_
  41.8 0.0 collective-permute-done.refs_4_.refs_2_
  41.8 1.3 %collective-permute-start.4 = (f32[3,2,80,512]{3,2,1,0:T(8,128)}, f32[3,2,80,512]{3,2,1,0:T(8,128)}, u32[]{:S(2)}, u32[]{:S(2)}) collective-permute-start(f32[3,2,80,512]{3,2,1,0:T(8,128)} %get-tuple-element.12), channel_id=1, source_target_pairs={{1,2},{2,1},{3,4},{4,3},{5,6},{6,5},{7,8},{8,7},{9,10},{10,9},{11,... | collective-permute-start | bytes 2949128 | tf_op jit(solution)/shard_map/ppermute | solution.py:450
  43.1 2.8 %two_steps.3 = (f32[3,2,8,512]{3,2,1,0:T(8,128)}, f32[16,4,128]{2,1,0:T(4,128)}) custom-call(s32[1]{0:T(128)} %bitcast.refs_0_, f32[3,2,8,512]{3,2,1,0:T(8,128)} %seed.1.refs_1_, f32[3,2,256,512]{3,2,1,0:T(8,128)} %refs_1_.3, f32[3,2,8,512]{3,2,1,0:T(8,128)} %collective-permute-done.1.refs_3_, f32[3,2,256,512]{3,2,1,0:T(8,128)} %collective-permute-done.refs_4_.refs_2_, ...), custom_call_target="tpu_custom_call" | custom-call | flops 8000000 | bytes 480000 | tf_op jit(solution)/shard_map/two_steps/pallas_call | solution.py:400
  45.9 20.9 %all_to_all.11.new_ref = f32[16,4,128]{2,1,0:T(4,128)} all-to-all(f32[16,4,128]{2,1,0:T(4,128)} %get-tuple-element.14), channel_id=1, replica_groups=mesh['gx'=8,'gz'=16] {'gz'}, dimensions={0} | all-to-all | bytes 65536 | tf_op jit(solution)/shard_map/all_to_all | solution.py:453
  66.8 0.0 collective-permute-done.4.refs_5_.refs_3_
  66.9 1.9 %collective-permute-start.5 = (f32[3,2,72,512]{3,2,1,0:T(8,128)}, f32[3,2,72,512]{3,2,1,0:T(8,128)}, u32[]{:S(2)}, u32[]{:S(2)}) collective-permute-start(f32[3,2,72,512]{3,2,1,0:T(8,128)} %get-tuple-element.15), channel_id=1, source_target_pairs={{1,2},{2,1},{3,4},{4,3},{5,6},{6,5},{7,8},{8,7},{9,10},{10,9},{11,... | collective-permute-start | bytes 2654216 | tf_op jit(solution)/shard_map/ppermute | solution.py:450
  68.7 5.8 %constrain.1 = f32[3,2,32,4096]{3,2,1,0:T(8,128)} custom-call(f32[3,2,32,4096]{3,2,1,0:T(8,128)} %vel_ref.3, s32[2,32,4096]{2,1,0:T(8,128)} %ids_ref.3, s32[2,32,4096]{2,1,0:T(8,128)} %fluid_ref.3, f32[16,4,128]{2,1,0:T(4,128)} %all_to_all.11.new_ref, f32[32,256]{1,0:T(8,128)} %get-tuple-element.17.mean_ref), custom_call_target="tpu_custom_call" | custom-call | flops 10000000 | bytes 20000000 | tf_op jit(solution)/shard_map/constrain/pallas_call | solution.py:223
  74.5 9.0 %two_steps.4.refs_6_ = f32[3,2,256,512]{3,2,1,0:T(8,128)} custom-call(s32[1]{0:T(128)} %bitcast.refs_0_, f32[3,2,256,512]{3,2,1,0:T(8,128)} %refs_1_.3, f32[3,2,256,512]{3,2,1,0:T(8,128)} %collective-permute-done.refs_4_.refs_2_, f32[3,2,8,512]{3,2,1,0:T(8,128)} %collective-permute-done.2.refs_5_.refs_3_, ...), custom_call_target="tpu_custom_call" | custom-call | flops 168000000 | bytes 10080000 | tf_op jit(solution)/shard_map/two_steps/pallas_call | solution.py:400
  83.5 5.6 %collective-permute-done.5.refs_4_ = f32[3,2,72,512]{3,2,1,0:T(8,128)} collective-permute-done((f32[3,2,72,512]{3,2,1,0:T(8,128)}, f32[3,2,72,512]{3,2,1,0:T(8,128)}, u32[]{:S(2)}, u32[]{:S(2)}) %collective-permute-start.5) | collective-permute-done | bytes 884768 | tf_op jit(solution)/shard_map/ppermute | solution.py:450
  89.1 5.4 %two_steps.5 = f32[3,2,256,512]{3,2,1,0:T(8,128)} custom-call(s32[1]{0:T(128)} %bitcast.refs_0_, f32[3,2,256,512]{3,2,1,0:T(8,128)} %refs_1_.3, f32[3,2,256,512]{3,2,1,0:T(8,128)} %collective-permute-done.refs_4_.refs_2_, f32[3,2,80,512]{3,2,1,0:T(8,128)} %collective-permute-done.4.refs_5_.refs_3_, ...), custom_call_target="tpu_custom_call", output_to_operand_aliasing={{}: (6, {})} | custom-call | flops 80000000 | bytes 4800000 | tf_op jit(solution)/shard_map/two_steps/pallas_call | solution.py:400
Async XLA Ops:
  0.6 41.2 %collective-permute-start = (f32[3,2,256,512]{3,2,1,0:T(8,128)}, f32[3,2,256,512]{3,2,1,0:T(8,128)}, u32[]{:S(2)}, u32[]{:S(2)}) collective-permute-start(f32[3,2,256,512]{3,2,1,0:T(8,128)} %refs_1_.3), channel_id=1, source_target_pairs={{0,1},{1,0},{2,3},{3,2},{4,5},{5,4},{6,7},{7,6},{8,9},{9,8},{10,11... | collective-permute-start | bytes 9437192 | tf_op jit(solution)/shard_map/ppermute | solution.py:447
  3.8 38.0 %collective-permute-start.3 = (f32[3,2,96,512]{3,2,1,0:T(8,128)}, f32[3,2,96,512]{3,2,1,0:T(8,128)}, u32[]{:S(2)}, u32[]{:S(2)}) collective-permute-start(f32[3,2,96,512]{3,2,1,0:T(8,128)} %slice.3), channel_id=1, source_target_pairs={{1,2},{2,1},{3,4},{4,3},{5,6},{6,5},{7,8},{8,7},{9,10},{10,9},{11,... | collective-permute-start | bytes 3538952 | tf_op jit(solution)/shard_map/ppermute | solution.py:450
  36.6 5.3 %collective-permute-start.2 = (f32[3,2,8,512]{3,2,1,0:T(8,128)}, f32[3,2,8,512]{3,2,1,0:T(8,128)}, u32[]{:S(2)}, u32[]{:S(2)}) collective-permute-start(f32[3,2,8,512]{3,2,1,0:T(8,128)} %seed.1.refs_1_), channel_id=1, source_target_pairs={{1,2},{2,1},{3,4},{4,3},{5,6},{6,5},{7,8},{8,7},{9,10},{10,9},{11,... | collective-permute-start | bytes 294920 | tf_op jit(solution)/shard_map/ppermute | solution.py:450
  37.2 4.6 %collective-permute-start.1 = (f32[3,2,8,512]{3,2,1,0:T(8,128)}, f32[3,2,8,512]{3,2,1,0:T(8,128)}, u32[]{:S(2)}, u32[]{:S(2)}) collective-permute-start(f32[3,2,8,512]{3,2,1,0:T(8,128)} %seed.1.refs_1_), channel_id=1, source_target_pairs={{0,1},{1,0},{2,3},{3,2},{4,5},{5,4},{6,7},{7,6},{8,9},{9,8},{10,11... | collective-permute-start | bytes 294920 | tf_op jit(solution)/shard_map/ppermute | solution.py:447
  41.8 25.0 %collective-permute-start.4 = (f32[3,2,80,512]{3,2,1,0:T(8,128)}, f32[3,2,80,512]{3,2,1,0:T(8,128)}, u32[]{:S(2)}, u32[]{:S(2)}) collective-permute-start(f32[3,2,80,512]{3,2,1,0:T(8,128)} %get-tuple-element.12), channel_id=1, source_target_pairs={{1,2},{2,1},{3,4},{4,3},{5,6},{6,5},{7,8},{8,7},{9,10},{10,9},{11,... | collective-permute-start | bytes 2949128 | tf_op jit(solution)/shard_map/ppermute | solution.py:450
  66.9 22.3 %collective-permute-start.5 = (f32[3,2,72,512]{3,2,1,0:T(8,128)}, f32[3,2,72,512]{3,2,1,0:T(8,128)}, u32[]{:S(2)}, u32[]{:S(2)}) collective-permute-start(f32[3,2,72,512]{3,2,1,0:T(8,128)} %get-tuple-element.15), channel_id=1, source_target_pairs={{1,2},{2,1},{3,4},{4,3},{5,6},{6,5},{7,8},{8,7},{9,10},{10,9},{11,... | collective-permute-start | bytes 2654216 | tf_op jit(solution)/shard_map/ppermute | solution.py:450
